TPU v7x, 256 devices: a whole 4x4x8 slice. The times are simulated.
256 devices in a mesh: pipe: 8 (over x, core), expert: 32 (over z, y).
Axes of the slice: x: 4, y: 4, z: 8, core: 2. Of those that a mesh axis runs over, the one named last changes fastest.
Arguments:
- forward_in: bfloat16 [8, 4096, 3584], P('pipe', 'expert'), may hold values from -6 to 6
- forward_route: int32 [8, 4096, 1], P('pipe', 'expert'), may hold values from 0 to 7; in each aligned block of 128 rows (0 to 127, 128 to 255, ..., all dimensions but the last counted through in order) at most 20 rows name the same one
- forward_share: float32 [8, 4096, 1], P('pipe', 'expert'), may hold values from 0.2 to 1
- backward_in: bfloat16 [8, 4096, 3584], P('pipe', 'expert'), may hold values from -6 to 6
- backward_grad: bfloat16 [8, 4096, 3584], P('pipe', 'expert'), may hold values from -6 to 6
- backward_route: int32 [8, 4096, 1], P('pipe', 'expert'), may hold values from 0 to 7; in each aligned block of 128 rows (0 to 127, 128 to 255, ..., all dimensions but the last counted through in order) at most 20 rows name the same one
- backward_share: float32 [8, 4096, 1], P('pipe', 'expert'), may hold values from 0.2 to 1
- norm_gain: float32 [8, 3584], P('pipe'), may hold values from 0.25 to 1.75
- gate_matrix: bfloat16 [8, 3584, 8192], P('pipe', None, 'expert'), may hold values from -0.09375 to 0.09375
- up_matrix: bfloat16 [8, 3584, 8192], P('pipe', None, 'expert'), may hold values from -0.09375 to 0.09375
- down_matrix: bfloat16 [8, 8192, 3584], P('pipe', 'expert'), may hold values from -0.1875 to 0.1875
Outputs:
- next_forward: bfloat16 [8, 4096, 3584], P('pipe', 'expert')
- next_backward: bfloat16 [8, 4096, 3584], P('pipe', 'expert')
Inputs may be any that keep to these rules, and one draw needn't show every extreme that they name: `forward_route`: each row names exactly one expert of its section. Among the rows of one device (aligned blocks of 128 rows) no expert is named more than 20 times, a bound that some block reaches. `backward_route`: as for forward_route.
All inputs are finite; a program needn't handle non-finite values.
Results may differ from a plain program's by a relative error of at most 0.0058.
Values may be sent and summed in bfloat16 or wider, within the bound.
A program may use at most 128 MiB of HBM per device.

v0:
```python
from functools import partial

import jax
import jax.numpy as jnp
from jax import lax
from jax.sharding import PartitionSpec as P

SLICES = 4


def passed_along(block, axis, distance):
    devices = range(lax.axis_size(axis))
    route = [((i - distance) % len(devices), i) for i in devices]
    return lax.ppermute(block, axis, route)


def normalize(values, gain_row):
    floats = values.astype(jnp.float32)
    scale_row = lax.rsqrt(jnp.mean(floats * floats, axis=-1, keepdims=True) + 1e-06)
    return (floats * scale_row * gain_row).astype(jnp.bfloat16)


def norm_backward(values, gain_row, d_normed):
    floats = values.astype(jnp.float32)
    scale_row = lax.rsqrt(jnp.mean(floats * floats, axis=-1, keepdims=True) + 1e-06)
    weighted = gain_row * d_normed
    return scale_row * weighted - floats * scale_row**3 * jnp.mean(
        floats * weighted, axis=-1, keepdims=True
    )


def slot_layout(route_rows, experts, capacity):
    pair_experts = route_rows.reshape(-1)
    onehot = (pair_experts[:, None] == jnp.arange(experts, dtype=jnp.int32)[None, :]).astype(
        jnp.int32
    )
    rank_in_expert = jnp.sum((jnp.cumsum(onehot, axis=0) - 1) * onehot, axis=1)
    return pair_experts * capacity + rank_in_expert


def forward_expert(expert_rows, gate_local, up_local, down_local):
    pre_gate = jnp.dot(expert_rows, gate_local, preferred_element_type=jnp.float32)
    pre_up = jnp.dot(expert_rows, up_local, preferred_element_type=jnp.float32)
    hidden = (jax.nn.silu(pre_gate) * pre_up).astype(jnp.bfloat16)
    return jnp.dot(hidden, down_local, preferred_element_type=jnp.float32).astype(jnp.bfloat16)


def backward_expert(joined, gate_local, up_local, down_local):
    half_width = joined.shape[-1] // 2
    expert_rows = joined[:, :half_width]
    expert_grads = joined[:, half_width:]
    contract = (((1,), (1,)), ((), ()))
    pre_gate = jnp.dot(expert_rows, gate_local, preferred_element_type=jnp.float32)
    pre_up = jnp.dot(expert_rows, up_local, preferred_element_type=jnp.float32)
    sigmoid_gate = jax.nn.sigmoid(pre_gate)
    d_hidden = lax.dot_general(
        expert_grads, down_local, contract, preferred_element_type=jnp.float32
    )
    d_gate = (d_hidden * pre_up * sigmoid_gate * (1.0 + pre_gate * (1.0 - sigmoid_gate))).astype(
        jnp.bfloat16
    )
    d_up = (d_hidden * pre_gate * sigmoid_gate).astype(jnp.bfloat16)
    running_sum = lax.dot_general(d_gate, gate_local, contract, preferred_element_type=jnp.float32)
    running_sum = running_sum + lax.dot_general(
        d_up, up_local, contract, preferred_element_type=jnp.float32
    )
    return running_sum.astype(jnp.bfloat16)


def through_experts(packed, expert_fn, experts, capacity):
    feature = packed.shape[-1]
    outgoing = jnp.repeat(packed, SLICES, axis=0)
    received = lax.all_to_all(outgoing, "expert", split_axis=0, concat_axis=0, tiled=True)
    result = expert_fn(received.reshape(-1, feature))
    result = result.reshape(received.shape[:2] + (result.shape[-1],))
    returned = lax.all_to_all(result, "expert", split_axis=0, concat_axis=0, tiled=True)
    model_width = returned.shape[-1]
    summed = jnp.sum(
        returned.reshape(experts, SLICES, capacity, model_width).astype(jnp.float32), axis=1
    )
    rounded = lax.optimization_barrier(summed.astype(jnp.bfloat16))
    return rounded.reshape(experts * capacity, model_width)


def per_device(
    forward_in,
    forward_route,
    forward_share,
    backward_in,
    backward_grad,
    backward_route,
    backward_share,
    norm_gain,
    gate_matrix,
    up_matrix,
    down_matrix,
):
    devices = lax.axis_size("expert")
    experts = devices // SLICES
    tokens = forward_in.shape[1]
    top_count = forward_route.shape[2]
    feature_width = forward_in.shape[2]
    capacity = SLICES * ((tokens * top_count * 5 // 4 + devices - 1) // devices)
    slot_count = experts * capacity
    gain_row = norm_gain[0]
    gate_local = gate_matrix[0]
    up_local = up_matrix[0]
    down_local = down_matrix[0]
    slot_ids = jnp.arange(slot_count, dtype=jnp.int32)
    section_input = forward_in[0]
    position = slot_layout(forward_route[0], experts, capacity)
    normed = normalize(section_input, gain_row)
    placing = (slot_ids[:, None] == position[None, :]).astype(jnp.bfloat16)
    packed = jnp.dot(
        placing, jnp.repeat(normed, top_count, axis=0), preferred_element_type=jnp.float32
    ).astype(jnp.bfloat16)
    expert_fn = partial(
        forward_expert, gate_local=gate_local, up_local=up_local, down_local=down_local
    )
    expert_out = through_experts(
        packed.reshape(experts, capacity, feature_width), expert_fn, experts, capacity
    )
    picked = expert_out[position].astype(jnp.float32) * forward_share[0].reshape(-1)[:, None]
    mixed_rows = section_input.astype(jnp.float32) + jnp.sum(
        picked.reshape(tokens, top_count, feature_width), axis=1
    )
    next_forward = passed_along(mixed_rows.astype(jnp.bfloat16)[None], "pipe", 1)
    saved_input = backward_in[0]
    section_grad = backward_grad[0]
    back_position = slot_layout(backward_route[0], experts, capacity)
    normed_back = normalize(saved_input, gain_row)
    back_mask = slot_ids[:, None] == back_position[None, :]
    back_placing = back_mask.astype(jnp.bfloat16)
    slot_share = jnp.sum(jnp.where(back_mask, backward_share[0].reshape(-1)[None, :], 0.0), axis=1)
    packed_back = jnp.dot(
        back_placing, jnp.repeat(normed_back, top_count, axis=0), preferred_element_type=jnp.float32
    ).astype(jnp.bfloat16)
    placed_grad = jnp.dot(
        back_placing,
        jnp.repeat(section_grad, top_count, axis=0),
        preferred_element_type=jnp.float32,
    )
    packed_grad = (placed_grad * slot_share[:, None]).astype(jnp.bfloat16)
    joined = jnp.concatenate([packed_back, packed_grad], axis=-1).reshape(
        experts, capacity, 2 * feature_width
    )
    back_fn = partial(
        backward_expert, gate_local=gate_local, up_local=up_local, down_local=down_local
    )
    d_out = through_experts(joined, back_fn, experts, capacity)
    d_normed = jnp.sum(
        d_out[back_position].astype(jnp.float32).reshape(tokens, top_count, feature_width), axis=1
    )
    d_input = section_grad.astype(jnp.float32) + norm_backward(saved_input, gain_row, d_normed)
    next_backward = passed_along(d_input.astype(jnp.bfloat16)[None], "pipe", -1)
    return (next_forward, next_backward)


def solution(mesh):
    return jax.shard_map(
        per_device,
        mesh=mesh,
        in_specs=(
            P("pipe", "expert", None),
            P("pipe", "expert", None),
            P("pipe", "expert", None),
            P("pipe", "expert", None),
            P("pipe", "expert", None),
            P("pipe", "expert", None),
            P("pipe", "expert", None),
            P("pipe", None),
            P("pipe", None, "expert"),
            P("pipe", None, "expert"),
            P("pipe", "expert", None),
        ),
        out_specs=(P("pipe", "expert", None), P("pipe", "expert", None)),
        check_vma=False,
    )
```

profile of v0, /device:TPU:1, one launch (start us, length us, event | category | flops | bytes accessed | tf_op | source)
XLA Modules:
  0.0 710.1 jit_solution(16290698024106419306)
XLA Ops:
  5.4 2.7 convolution_convert_fusion.2
  9.5 2.9 broadcast_in_dim.14
  12.4 12.3 %all-to-all-start = ((bf16[32,20,3584]{2,1,0:T(8,128)(2,1)}), bf16[32,20,3584]{2,1,0:T(8,128)(2,1)}, u32[]{:S(2)}, u32[]{:S(2)}) async-start(bf16[32,20,3584]{2,1,0:T(8,128)(2,1)} %bitcast.110), calls=%async_computation | async-start | bytes 11010048 | tf_op jit(solution)/shard_map/all_to_all | solution.py:73
  29.4 4.2 reshape.271
  33.6 111.2 %all-to-all-done = bf16[32,20,3584]{2,1,0:T(8,128)(2,1)} async-done(((bf16[32,20,3584]{2,1,0:T(8,128)(2,1)}), bf16[32,20,3584]{2,1,0:T(8,128)(2,1)}, u32[]{:S(2)}, u32[]{:S(2)}) %all-to-all-start) | async-done | bytes 4587552 | tf_op jit(solution)/shard_map/all_to_all | solution.py:73
  144.7 7.2 %broadcast_in_dim.22 = bf16[8,4,20,7168]{3,2,1,0:T(8,128)(2,1)} broadcast(bf16[8,20,7168]{2,1,0:T(8,128)(2,1)} %reshape.271), dimensions={0,2,3} | broadcast | bytes 11468800 | tf_op jit(solution)/shard_map/broadcast_in_dim | solution.py:72
  151.9 12.9 %all-to-all-start.2 = ((bf16[32,20,7168]{2,1,0:T(8,128)(2,1)}), bf16[32,20,7168]{2,1,0:T(8,128)(2,1)}, u32[]{:S(2)}, u32[]{:S(2)}) async-start(bf16[32,20,7168]{2,1,0:T(8,128)(2,1)} %bitcast.109), calls=%async_computation.2 | async-start | bytes 22020096 | tf_op jit(solution)/shard_map/all_to_all | solution.py:73
  164.8 7.3 %reshape.267 = bf16[640,3584]{1,0:T(8,128)(2,1)} reshape(bf16[32,20,3584]{2,1,0:T(8,128)(2,1)} %all-to-all-done) | data formatting | bytes 9175040 | tf_op jit(solution)/shard_map/reshape | solution.py:74
  172.1 4.2 fusion.35
  176.3 9.8 %convolution_convert_fusion = bf16[640,3584]{1,0:T(8,128)(2,1)} fusion(bf16[1,256,3584]{2,1,0:T(8,128)(2,1)} %param.21, bf16[640,3584]{1,0:T(8,128)(2,1)} %reshape.267, bf16[1,3584,256]{2,1,0:T(8,128)(2,1)S(1)} %copy-done, f32[640,256]{1,0:T(8,128)S(1)} %fusion.35), kind=kOutput, calls=%fused_computation.3 | convolution fusion | flops 2352087040 | bytes 13500416 | tf_op jit(solution)/shard_map/dot_general | solution.py:45
  186.1 7.3 %reshape.268 = bf16[32,20,3584]{2,1,0:T(8,128)(2,1)} reshape(bf16[640,3584]{1,0:T(8,128)(2,1)} %convolution_convert_fusion) | data formatting | bytes 9175040 | tf_op jit(solution)/shard_map/reshape | solution.py:75
  193.4 216.1 %all-to-all-done.2 = bf16[32,20,7168]{2,1,0:T(8,128)(2,1)} async-done(((bf16[32,20,7168]{2,1,0:T(8,128)(2,1)}), bf16[32,20,7168]{2,1,0:T(8,128)(2,1)}, u32[]{:S(2)}, u32[]{:S(2)}) %all-to-all-start.2) | async-done | bytes 9175072 | tf_op jit(solution)/shard_map/all_to_all | solution.py:73
  409.5 19.3 %all-to-all-start.1 = ((bf16[32,20,3584]{2,1,0:T(8,128)(2,1)}), bf16[32,20,3584]{2,1,0:T(8,128)(2,1)}, u32[]{:S(2)}, u32[]{:S(2)}) async-start(bf16[32,20,3584]{2,1,0:T(8,128)(2,1)} %reshape.268), calls=%async_computation.1 | async-start | bytes 11010048 | tf_op jit(solution)/shard_map/all_to_all | solution.py:76
  428.8 13.4 %reshape.273 = bf16[640,7168]{1,0:T(8,128)(2,1)} reshape(bf16[32,20,7168]{2,1,0:T(8,128)(2,1)} %all-to-all-done.2) | data formatting | bytes 18350080 | tf_op jit(solution)/shard_map/reshape | solution.py:74
  442.2 4.4 fusion.1
  449.6 11.3 %fusion.32 = f32[640,3584]{1,0:T(8,128)} fusion(bf16[1,3584,256]{2,1,0:T(8,128)(2,1)} %param.19, f32[640,256]{1,0:T(8,128)S(1)} %fusion.1, bf16[1,3584,256]{2,1,0:T(8,128)(2,1)S(1)} %copy-done, bf16[640,7168]{1,0:T(8,128)(2,1)} %reshape.273, f32[640,256]{1,0:T(8,128)S(1)} %fusion.3), kind=kOutput, calls=%fused_computation.49 | convolution fusion | flops 2350448640 | bytes 18743296 | tf_op jit(solution)/shard_map/dot_general | solution.py:63
  460.8 7.1 add_convert_fusion
  467.9 7.2 %reshape.274 = bf16[32,20,3584]{2,1,0:T(8,128)(2,1)} reshape(bf16[640,3584]{1,0:T(8,128)(2,1)} %add_convert_fusion) | data formatting | bytes 9175040 | tf_op jit(solution)/shard_map/reshape | solution.py:75
  475.1 73.1 %all-to-all-done.1 = bf16[32,20,3584]{2,1,0:T(8,128)(2,1)} async-done(((bf16[32,20,3584]{2,1,0:T(8,128)(2,1)}), bf16[32,20,3584]{2,1,0:T(8,128)(2,1)}, u32[]{:S(2)}, u32[]{:S(2)}) %all-to-all-start.1) | async-done | bytes 4587552 | tf_op jit(solution)/shard_map/all_to_all | solution.py:76
  548.3 11.4 %all-to-all-start.3 = ((bf16[32,20,3584]{2,1,0:T(8,128)(2,1)}), bf16[32,20,3584]{2,1,0:T(8,128)(2,1)}, u32[]{:S(2)}, u32[]{:S(2)}) async-start(bf16[32,20,3584]{2,1,0:T(8,128)(2,1)} %reshape.274), calls=%async_computation.3 | async-start | bytes 11010048 | tf_op jit(solution)/shard_map/all_to_all | solution.py:76
  559.7 4.9 bitcast_reduce_fusion.1
  566.1 2.0 gather_fusion
  568.2 2.7 fusion.15
  570.9 2.9 collective-permute-start
  573.8 105.1 %all-to-all-done.3 = bf16[32,20,3584]{2,1,0:T(8,128)(2,1)} async-done(((bf16[32,20,3584]{2,1,0:T(8,128)(2,1)}), bf16[32,20,3584]{2,1,0:T(8,128)(2,1)}, u32[]{:S(2)}, u32[]{:S(2)}) %all-to-all-start.3) | async-done | bytes 4587552 | tf_op jit(solution)/shard_map/all_to_all | solution.py:76
  678.9 5.0 bitcast_reduce_fusion
  685.4 2.0 gather_fusion.1
  687.4 2.0 fusion.19
  689.4 1.9 fusion.23
  691.3 3.5 collective-permute-start.1
  694.8 12.2 %collective-permute-done.1 = bf16[1,128,3584]{2,1,0:T(8,128)(2,1)S(1)} collective-permute-done((bf16[1,128,3584]{2,1,0:T(8,128)(2,1)S(1)}, bf16[1,128,3584]{2,1,0:T(8,128)(2,1)S(1)}, u32[]{:S(2)}, u32[]{:S(2)}) %collective-permute-start.1) | collective-permute-done | bytes 917536 | tf_op jit(solution)/shard_map/ppermute | solution.py:14
  707.0 2.2 copy.15
  (48 shorter events, 17.6 us)
Async XLA Ops:
  0.6 175.7 %copy-start = (bf16[1,3584,256]{2,1,0:T(8,128)(2,1)S(1)}, bf16[1,3584,256]{2,1,0:T(8,128)(2,1)}, u32[]{:S(2)}) copy-start(bf16[1,3584,256]{2,1,0:T(8,128)(2,1)} %param.20) | copy-start | bytes 5505028
  12.4 12.3 %copy-start.6 = (s32[1,128,1]{1,2,0:T(1,128)S(1)}, s32[1,128,1]{1,2,0:T(1,128)}, u32[]{:S(2)}) copy-start(s32[1,128,1]{1,2,0:T(1,128)} %param.16) | copy-start | bytes 1540
  12.4 12.8 %copy-start.9 = (f32[1,128,1]{1,2,0:T(1,128)S(1)}, f32[1,128,1]{1,2,0:T(1,128)}, u32[]{:S(2)}) copy-start(f32[1,128,1]{1,2,0:T(1,128)} %param.17) | copy-start | bytes 1540
  12.4 12.9 %copy-start.2 = (bf16[1,128,3584]{2,1,0:T(8,128)(2,1)S(1)}, bf16[1,128,3584]{2,1,0:T(8,128)(2,1)}, u32[]{:S(2)}) copy-start(bf16[1,128,3584]{2,1,0:T(8,128)(2,1)} %param.14) | copy-start | bytes 2752516
  12.4 132.3 %all-to-all-start = ((bf16[32,20,3584]{2,1,0:T(8,128)(2,1)}), bf16[32,20,3584]{2,1,0:T(8,128)(2,1)}, u32[]{:S(2)}, u32[]{:S(2)}) async-start(bf16[32,20,3584]{2,1,0:T(8,128)(2,1)} %bitcast.110), calls=%async_computation | async-start | bytes 11010048 | tf_op jit(solution)/shard_map/all_to_all | solution.py:73
  151.9 257.6 %all-to-all-start.2 = ((bf16[32,20,7168]{2,1,0:T(8,128)(2,1)}), bf16[32,20,7168]{2,1,0:T(8,128)(2,1)}, u32[]{:S(2)}, u32[]{:S(2)}) async-start(bf16[32,20,7168]{2,1,0:T(8,128)(2,1)} %bitcast.109), calls=%async_computation.2 | async-start | bytes 22020096 | tf_op jit(solution)/shard_map/all_to_all | solution.py:73
  409.5 138.7 %all-to-all-start.1 = ((bf16[32,20,3584]{2,1,0:T(8,128)(2,1)}), bf16[32,20,3584]{2,1,0:T(8,128)(2,1)}, u32[]{:S(2)}, u32[]{:S(2)}) async-start(bf16[32,20,3584]{2,1,0:T(8,128)(2,1)} %reshape.268), calls=%async_computation.1 | async-start | bytes 11010048 | tf_op jit(solution)/shard_map/all_to_all | solution.py:76
  442.2 5.5 copy-start.1
  442.2 6.0 copy-start.5
  475.1 84.6 %copy-start.7 = (s32[1,128,1]{1,2,0:T(1,128)S(1)}, s32[1,128,1]{1,2,0:T(1,128)}, u32[]{:S(2)}) copy-start(s32[1,128,1]{1,2,0:T(1,128)} %param.12) | copy-start | bytes 1540
  548.3 130.7 %all-to-all-start.3 = ((bf16[32,20,3584]{2,1,0:T(8,128)(2,1)}), bf16[32,20,3584]{2,1,0:T(8,128)(2,1)}, u32[]{:S(2)}, u32[]{:S(2)}) async-start(bf16[32,20,3584]{2,1,0:T(8,128)(2,1)} %reshape.274), calls=%async_computation.3 | async-start | bytes 11010048 | tf_op jit(solution)/shard_map/all_to_all | solution.py:76
  566.1 2.1 copy-start.8
  570.9 123.9 %collective-permute-start = (bf16[1,128,3584]{2,1,0:T(8,128)(2,1)}, bf16[1,128,3584]{2,1,0:T(8,128)(2,1)}, u32[]{:S(2)}, u32[]{:S(2)}) collective-permute-start(bf16[1,128,3584]{2,1,0:T(8,128)(2,1)} %fusion.15), channel_id=1, source_target_pairs={{224,0},{0,32},{32,64},{64,96},{96,128},{128,160},{160,192},{192,2... | collective-permute-start | bytes 2752520 | tf_op jit(solution)/shard_map/ppermute | solution.py:14
  687.4 2.0 copy-start.3
  687.4 2.0 copy-start.4
  691.3 15.7 %collective-permute-start.1 = (bf16[1,128,3584]{2,1,0:T(8,128)(2,1)S(1)}, bf16[1,128,3584]{2,1,0:T(8,128)(2,1)S(1)}, u32[]{:S(2)}, u32[]{:S(2)}) collective-permute-start(bf16[1,128,3584]{2,1,0:T(8,128)(2,1)S(1)} %fusion.23), channel_id=1, source_target_pairs={{32,0},{64,32},{96,64},{128,96},{160,128},{192,160},{224,192},{0,2... | collective-permute-start | bytes 2752520 | tf_op jit(solution)/shard_map/ppermute | solution.py:14
where the time goes:
time: 714 us; the launch traced here: 710 us
  waiting for transfers between devices  518 us (73%)
  local copies, waits for them, and re-layouts  62.5 us (9%)
  starting transfers between devices  62.2 us (9%)
  matrix products  43 us (6%)
  other arithmetic  23.7 us (3%)
    all_to_all x2, waiting for transfers between devices, through_experts(): lax.all_to_all(outgoing, 'expert', split_axis=0, concat_axis=0, tiled=True)  327 us
    all_to_all x2, waiting for transfers between devices, through_experts(): lax.all_to_all(result, 'expert', split_axis=0, concat_axis=0, tiled=True)  178 us
    all_to_all x2, starting transfers between devices, through_experts(): lax.all_to_all(result, 'expert', split_axis=0, concat_axis=0, tiled=True)  30.6 us
    all_to_all x2, starting transfers between devices, through_experts(): lax.all_to_all(outgoing, 'expert', split_axis=0, concat_axis=0, tiled=True)  25.2 us
    reshape x2, local copies, waits for them, and re-layouts, through_experts(): result = expert_fn(received.reshape(-1, feature))  20.7 us
    reshape x2, local copies, waits for them, and re-layouts, through_experts(): result = result.reshape(received.shape[:2] + (result.shape[-1],))  14.5 us
  transfers between devices with their start and end apart: 6, of which 5 were waited for; matrix products, arithmetic and copies ran while one was open for 15% of the time, Pallas kernels for 0%

commit v1 on v0

v1 whole, which is shorter than its diff:
```python
import jax
import jax.numpy as jnp
from jax import lax
from jax.experimental import pallas as pl
from jax.experimental.pallas import tpu as pltpu
from jax.sharding import PartitionSpec as P

MESH = pl.DeviceIdType.MESH
NP, NZ, NY = 8, 8, 4
T = 128
D = 3584
C = 896
W = D + C
H = 256
KC = 512
NK = D // KC
F32, BF16 = jnp.float32, jnp.bfloat16
ORDER = (4, 3, 5, 2, 6, 1, 7)
NEAR = (1, 7, 2, 6, 3, 5, 4)


def dot_nn(a, b):
    return lax.dot_general(a, b, (((1,), (0,)), ((), ())), preferred_element_type=F32)


def dot_nt(a, b):
    return lax.dot_general(a, b, (((1,), (1,)), ((), ())), preferred_element_type=F32)


def iota(shape, dim):
    return lax.broadcasted_iota(jnp.int32, shape, dim)


def slots_of(route_row):
    onehot = (iota((16, T), 0) == route_row).astype(F32)
    before = (iota((T, T), 0) < iota((T, T), 1)).astype(F32).astype(BF16)
    count = dot_nn(onehot.astype(BF16), before)
    rank = jnp.sum(count * onehot, axis=0, keepdims=True)
    base = route_row.astype(F32) * 16.0
    main = jnp.where(rank < 15.5, base + rank, -1000.0)
    extra = jnp.where(rank < 15.5, -1000.0, base + rank - 16.0)
    return main, extra


def placing(slot_row):
    return (iota((T, T), 0).astype(F32) == slot_row).astype(F32)


def column(row):
    return jnp.transpose(jnp.broadcast_to(row, (T, T)))[:, 0:1]


def unfold(k):
    m, n = iota((32, T), 0), iota((32, T), 1)
    return (n == (m >> 2) * 16 + (m & 3) + 4 * k).astype(F32).astype(BF16)


def fold(k):
    n, m = iota((T, 32), 0), iota((T, 32), 1)
    return (n == (m >> 2) * 16 + (m & 3) + 4 * k).astype(F32).astype(BF16)


def kernel(
    fin, froute, fshare, bin_, bgrad, broute, bshare, gain, gate, up, down,
    nf, nb,
    xin, shp, meta_s, meta_r, gain_s, gain_r, send, recv, pair, extra,
    gate_o, up_o, down_o, gate_r, up_r, down_r,
    acc, hid, part_s, part_r, own, eo_b, eo_f, ret_s, ret_r, qbuf,
    lsem, zs, zr, ys, yr, ws, wr, ps, pr, rs, rr, xs, xr,
):
    p = lax.axis_index("pipe")
    i = lax.axis_index("expert")
    z, y = i // NY, i % NY
    core = p % 2
    nxt, prv = (p + 1) % NP, (p + NP - 1) % NP
    ya = y + 1 - 2 * (y % 2)
    yb = (y + NY - 1 + 2 * (y % 2)) % NY
    yt = ya * (1 - core) + yb * core
    yw = ya * core + yb * (1 - core)

    def at_z(pp, zz):
        return (pp, zz * NY + y)

    tok = (p, z * NY + yt)
    wgt = (p, z * NY + yw)

    def remote(src, dst, s, r, device):
        return pltpu.make_async_remote_copy(
            src_ref=src, dst_ref=dst, send_sem=s, recv_sem=r, device_id=device, device_id_type=MESH
        )

    bar = pltpu.get_barrier_semaphore()

    def greet(d, _):
        pl.semaphore_signal(bar, inc=1, device_id=at_z(nxt, (z + d) % NZ), device_id_type=MESH)
        pl.semaphore_signal(bar, inc=1, device_id=at_z(prv, (z + d) % NZ), device_id_type=MESH)
        return 0

    def greet_own(d, _):
        pl.semaphore_signal(bar, inc=1, device_id=at_z(p, (z + d) % NZ), device_id_type=MESH)
        return 0

    lax.fori_loop(0, NZ, greet, 0)
    lax.fori_loop(1, NZ, greet_own, 0)
    pl.semaphore_signal(bar, inc=1, device_id=tok, device_id_type=MESH)
    pl.semaphore_signal(bar, inc=1, device_id=wgt, device_id_type=MESH)

    loads = [
        pltpu.make_async_copy(bgrad.at[0], xin.at[0], lsem.at[0]),
        pltpu.make_async_copy(bin_.at[0], xin.at[1], lsem.at[1]),
        pltpu.make_async_copy(fin.at[0], xin.at[2], lsem.at[2]),
        pltpu.make_async_copy(down.at[0], down_o, lsem.at[3]),
        pltpu.make_async_copy(gate.at[0], gate_o, lsem.at[4]),
        pltpu.make_async_copy(up.at[0], up_o, lsem.at[5]),
    ]
    for c in loads:
        c.start()

    def pack(j, main, ex, chunk):
        pm = placing(main).astype(BF16)
        folded = jnp.zeros((T, C), F32)
        for k in range(4):
            v = chunk(k)
            send[j, :, :, k * C:(k + 1) * C] = dot_nn(pm, v).astype(BF16).reshape(NZ, 16, C)
            folded = folded + dot_nn(placing(ex + 4.0 * k).astype(BF16), v)
        send[j, :, :, D:] = folded.astype(BF16).reshape(NZ, 16, C)

    def inv_rms(ref):
        total = jnp.zeros((T, 1), F32)
        for k in range(4):
            v = ref[:, k * C:(k + 1) * C].astype(F32)
            total = total + jnp.sum(v * v, axis=1, keepdims=True)
        return lax.rsqrt(total / D + 1e-6)

    def z_copy(j, d):
        return remote(send.at[j, (z + d) % NZ], recv.at[j, z], zs.at[j, d], zr.at[j, d], at_z(p, (z + d) % NZ))

    def z_send(j):
        for d in ORDER:
            z_copy(j, d).start()

    def relay_copy(j, d):
        src = (z - d + NZ) % NZ
        ref = send.at[j, src] if d == 0 else recv.at[j, src]
        return remote(ref, pair.at[j, src], ys.at[j, d], yr.at[j, d], tok)

    def relay(j, ds):
        for d in ds:
            if d:
                z_copy(j, d).wait_recv()
            relay_copy(j, d).start()

    def keep(j):
        return pltpu.make_async_copy(send.at[j, z], recv.at[j, z], lsem.at[6 + j])

    bmain, bextra = slots_of(broute[...])
    loads[0].wait()
    share_col = column(bshare[...])
    pack(0, bmain, bextra, lambda k: (share_col * xin[0, :, k * C:(k + 1) * C].astype(F32)).astype(BF16))
    pl.semaphore_wait(bar, 25)
    z_send(0)
    weight_copies = [
        remote(down.at[0], down_r, ws.at[0], wr.at[0], wgt),
        remote(gate.at[0], gate_r, ws.at[1], wr.at[1], wgt),
        remote(up.at[0], up_r, ws.at[2], wr.at[2], wgt),
    ]
    weight_copies[0].start()
    relay(0, (0,))
    keep(0).start()
    weight_copies[1].start()
    weight_copies[2].start()

    loads[1].wait()
    r_back = inv_rms(xin.at[1])
    pack(1, bmain, bextra, lambda k: (
        xin[1, :, k * C:(k + 1) * C].astype(F32) * r_back * gain[:, k * C:(k + 1) * C]).astype(BF16))
    z_send(1)
    relay(1, (0,))
    keep(1).start()

    fmain, fextra = slots_of(froute[...])
    loads[2].wait()
    r_fwd = inv_rms(xin.at[2])
    pack(2, fmain, fextra, lambda k: (
        xin[2, :, k * C:(k + 1) * C].astype(F32) * r_fwd * gain[:, k * C:(k + 1) * C]).astype(BF16))

    def rows(*parts):
        return jnp.concatenate(list(parts) + [jnp.zeros((8 - len(parts), T), F32)], axis=0)

    meta_s[0] = rows(bmain, bextra)
    meta_s[1] = rows(fmain, fextra, fshare[...])
    gain_s[...] = jnp.broadcast_to(gain[...], (8, D))
    down_pipe, up_pipe = (prv, i), (nxt, i)
    ship = [
        remote(meta_s.at[0], meta_r.at[0], xs.at[0], xr.at[0], down_pipe),
        remote(gain_s, gain_r, xs.at[1], xr.at[1], down_pipe),
        remote(xin.at[0], shp.at[0], xs.at[2], xr.at[2], down_pipe),
        remote(xin.at[1], shp.at[1], xs.at[3], xr.at[3], down_pipe),
        remote(meta_s.at[1], meta_r.at[1], xs.at[4], xr.at[4], up_pipe),
        remote(xin.at[2], shp.at[2], xs.at[5], xr.at[5], up_pipe),
    ]
    for c in ship:
        c.start()

    relay(0, NEAR)
    z_send(2)
    relay(2, (0,))
    keep(2).start()

    def gather_extra(j):
        for k in range(4):
            u = unfold(k)
            extra[j, 0:32, k * C:(k + 1) * C] = dot_nn(u, pair[j, :, :, D:].reshape(T, C)).astype(BF16)
            extra[j, 32:64, k * C:(k + 1) * C] = dot_nn(u, recv[j, :, :, D:].reshape(T, C)).astype(BF16)

    def all_rows(j, ds):
        return jnp.concatenate([
            pair[j, :, :, ds].reshape(T, KC), extra[j, 0:32, ds],
            recv[j, :, :, ds].reshape(T, KC), extra[j, 32:64, ds]], axis=0)

    def first(j, mats):
        for m, _, _ in mats:
            acc[m] = jnp.zeros((320, H), F32)

        def step(n, _):
            ds = pl.ds(pl.multiple_of(n * KC, KC), KC)
            v = all_rows(j, ds)
            for m, w, transposed in mats:
                acc[m] += dot_nt(v, w[:, ds]) if transposed else dot_nn(v, w[ds, :])
            return 0

        lax.fori_loop(0, NK, step, 0)

    def arrived(j):
        keep(j).wait()
        for d in range(NZ):
            relay_copy(j, d).wait_recv()
        gather_extra(j)

    def part_copy(b, n):
        if isinstance(n, int) and n == NK:
            ds = pl.ds(D, C)
        else:
            ds = pl.ds(pl.multiple_of(n * KC, KC), KC)
        return remote(part_s.at[b, :, :, ds], part_r.at[b, :, :, ds], ps.at[b, n], pr.at[b, n], tok)

    def second(b, out):
        def theirs(n, _):
            ds = pl.ds(pl.multiple_of(n * KC, KC), KC)
            o = out(slice(0, 160), ds).astype(BF16)
            part_s[b, :, :, ds] = o[:T].reshape(NZ, 16, KC)
            eo_b[:, ds] = o[T:]
            part_copy(b, n).start()
            return 0

        lax.fori_loop(0, NK, theirs, 0)

        def fold_extra(dst):
            folded = jnp.zeros((T, C), F32)
            for k in range(4):
                folded = folded + dot_nn(fold(k), eo_b[:, k * C:(k + 1) * C])
            dst[b, :, :, D:] = folded.astype(BF16).reshape(NZ, 16, C)

        fold_extra(part_s)
        part_copy(b, NK).start()

        def ours(n, _):
            ds = pl.ds(pl.multiple_of(n * KC, KC), KC)
            o = out(slice(160, 320), ds)
            own[:, ds] = o[:T]
            eo_f[:, ds] = o[T:]
            return 0

        lax.fori_loop(0, NK, ours, 0)

        def add(n, _):
            ds = pl.ds(pl.multiple_of(n * KC, KC), KC)
            part_copy(b, n).wait_recv()
            o = own[:, ds] + part_r[b, :, :, ds].reshape(T, KC).astype(F32)
            ret_s[b, :, :, ds] = o.astype(BF16).reshape(NZ, 16, KC)
            return 0

        lax.fori_loop(0, NK, add, 0)
        part_copy(b, NK).wait_recv()
        for k in range(4):
            ks = slice(k * C, (k + 1) * C)
            theirs_k = dot_nn(unfold(k), part_r[b, :, :, D:].reshape(T, C))
            eo_b[:, ks] = (eo_f[:, ks] + theirs_k).astype(BF16)
        fold_extra(ret_s)

    def ret_copy(b, d):
        zz = (z + d) % NZ
        return remote(ret_s.at[b, zz], ret_r.at[b, z], rs.at[b, d], rr.at[b, d], at_z(prv if b == 0 else nxt, zz))

    loads[3].wait()
    arrived(0)
    weight_copies[0].wait_recv()
    first(0, [(0, down_o, True), (1, down_r, True)])
    relay(1, NEAR)
    loads[4].wait()
    loads[5].wait()
    arrived(1)
    weight_copies[1].wait_recv()
    weight_copies[2].wait_recv()
    first(1, [(2, gate_o, False), (3, gate_r, False), (4, up_o, False), (5, up_r, False)])

    def act_back(n, _):
        ds = pl.ds(pl.multiple_of(n * 32, 32), 32)
        for s in range(2):
            dh, pg, pu = acc[s, ds], acc[2 + s, ds], acc[4 + s, ds]
            sg = jax.nn.sigmoid(pg)
            hid[s, ds] = (dh * pu * sg * (1.0 + pg * (1.0 - sg))).astype(BF16)
            hid[2 + s, ds] = (dh * pg * sg).astype(BF16)
        return 0

    lax.fori_loop(0, 10, act_back, 0)

    def out_back(rows_, ds):
        return (dot_nt(hid[0, rows_], gate_o[ds, :]) + dot_nt(hid[1, rows_], gate_r[ds, :])
                + dot_nt(hid[2, rows_], up_o[ds, :]) + dot_nt(hid[3, rows_], up_r[ds, :]))

    second(0, out_back)
    for d in (4, 3, 5, 2, 6, 1, 7, 0):
        ret_copy(0, d).start()

    relay(2, NEAR)
    arrived(2)
    first(2, [(2, gate_o, False), (3, gate_r, False), (4, up_o, False), (5, up_r, False)])

    def act_fwd(n, _):
        ds = pl.ds(pl.multiple_of(n * 32, 32), 32)
        for s in range(2):
            pg, pu = acc[2 + s, ds], acc[4 + s, ds]
            hid[s, ds] = (pg * jax.nn.sigmoid(pg) * pu).astype(BF16)
        return 0

    lax.fori_loop(0, 10, act_fwd, 0)

    def out_fwd(rows_, ds):
        return dot_nn(hid[0, rows_], down_o[:, ds]) + dot_nn(hid[1, rows_], down_r[:, ds])

    second(1, out_fwd)
    for d in (4, 3, 5, 2, 6, 1, 7, 0):
        ret_copy(1, d).start()

    for c in ship:
        c.wait()

    def take(b, main, ex, k):
        g = jnp.transpose(placing(main)).astype(BF16)
        ge = jnp.transpose(placing(ex + 4.0 * k)).astype(BF16)
        return (dot_nn(g, ret_r[b, :, :, k * C:(k + 1) * C].reshape(T, C))
                + dot_nn(ge, ret_r[b, :, :, D:].reshape(T, C)))

    for d in range(NZ):
        ret_copy(0, d).wait_recv()
    main, ex = meta_r[0, 0:1, :], meta_r[0, 1:2, :]
    r = inv_rms(shp.at[1])
    total = jnp.zeros((T, 1), F32)
    for k in range(4):
        ks = slice(k * C, (k + 1) * C)
        q = gain_r[0:1, ks] * take(0, main, ex, k)
        qbuf[:, ks] = q
        total = total + jnp.sum(shp[1, :, ks].astype(F32) * q, axis=1, keepdims=True)
    coef = r * r * r * (total / D)
    for k in range(4):
        ks = slice(k * C, (k + 1) * C)
        nb[0, :, ks] = (shp[0, :, ks].astype(F32) + (r * qbuf[:, ks] - shp[1, :, ks].astype(F32) * coef)).astype(BF16)

    for d in range(NZ):
        ret_copy(1, d).wait_recv()
    main, ex = meta_r[1, 0:1, :], meta_r[1, 1:2, :]
    share_fwd = column(meta_r[1, 2:3, :])
    for k in range(4):
        ks = slice(k * C, (k + 1) * C)
        nf[0, :, ks] = (shp[2, :, ks].astype(F32) + share_fwd * take(1, main, ex, k)).astype(BF16)

    for j in range(3):
        for d in range(NZ):
            if d:
                z_copy(j, d).wait_send()
            relay_copy(j, d).wait_send()
        weight_copies[j].wait_send()
    for b in range(2):
        for n in range(NK + 1):
            part_copy(b, n).wait_send()
        for d in range(NZ):
            ret_copy(b, d).wait_send()


def per_device(fin, froute, fshare, bin_, bgrad, broute, bshare, gain, gate, up, down):
    vm = pl.BlockSpec(memory_space=pltpu.VMEM)
    hbm = pl.BlockSpec(memory_space=pl.ANY)
    dma = pltpu.SemaphoreType.DMA
    out = jax.ShapeDtypeStruct((1, T, D), BF16)
    v = pltpu.VMEM
    return pl.pallas_call(
        kernel,
        out_shape=(out, out),
        in_specs=[hbm, vm, vm, hbm, hbm, vm, vm, vm, hbm, hbm, hbm],
        out_specs=(vm, vm),
        scratch_shapes=[
            v((3, T, D), BF16), v((3, T, D), BF16), v((2, 8, T), F32), v((2, 8, T), F32),
            v((8, D), F32), v((8, D), F32),
            v((3, NZ, 16, W), BF16), v((3, NZ, 16, W), BF16), v((3, NZ, 16, W), BF16), v((3, 64, D), BF16),
            v((D, H), BF16), v((D, H), BF16), v((H, D), BF16),
            v((D, H), BF16), v((D, H), BF16), v((H, D), BF16),
            v((6, 320, H), F32), v((4, 320, H), BF16),
            v((2, NZ, 16, W), BF16), v((2, NZ, 16, W), BF16),
            v((T, D), F32), v((32, D), BF16), v((32, D), F32),
            v((2, NZ, 16, W), BF16), v((2, NZ, 16, W), BF16), v((T, D), F32),
            dma((9,)), dma((3, NZ)), dma((3, NZ)), dma((3, NZ)), dma((3, NZ)),
            dma((3,)), dma((3,)), dma((2, NK + 1)), dma((2, NK + 1)),
            dma((2, NZ)), dma((2, NZ)), dma((6,)), dma((6,)),
        ],
        compiler_params=pltpu.CompilerParams(
            collective_id=1, has_side_effects=True, vmem_limit_bytes=60 << 20
        ),
        name="dualpipe_step",
    )(
        fin, froute.reshape(1, T), fshare.reshape(1, T), bin_, bgrad, broute.reshape(1, T),
        bshare.reshape(1, T), gain, gate, up, down,
    )


def solution(mesh):
    spec = P("pipe", "expert", None)
    return jax.shard_map(
        per_device,
        mesh=mesh,
        in_specs=(
            spec, spec, spec, spec, spec, spec, spec,
            P("pipe", None), P("pipe", None, "expert"), P("pipe", None, "expert"), P("pipe", "expert", None),
        ),
        out_specs=(spec, spec),
        check_vma=False,
    )
```

time: 714 us -> 185 us (0.26)
  waiting for transfers between devices: 518 us -> 0 us
  Pallas kernels: 0 us -> 181 us
  starting transfers between devices: 62.2 us -> 0 us
  local copies, waits for them, and re-layouts: 62.5 us -> 3.17 us
  matrix products: 43 us -> 0 us
  other arithmetic: 23.7 us -> 0 us
    all_to_all x4 -> x0, waiting for transfers between devices: 506 us -> none  [the longest x2 327 us: through_experts(): lax.all_to_all(outgoing, 'expert', split_axis=0, concat_axis=0, tiled=True)]
    pallas_call x0 -> x1, Pallas kernels: none -> 181 us  [per_device(): pl.pallas_call(kernel, out_shape=(out, out), in_specs=[hbm, vm, vm, hbm,...]
    all_to_all x4 -> x0, starting transfers between devices: 55.8 us -> none  [the longest x2 30.6 us: through_experts(): lax.all_to_all(result, 'expert', split_axis=0, concat_axis=0, tiled=True)]
    reshape x8 -> x0, local copies, waits for them, and re-layouts: 43.6 us -> none  [the longest x2 20.7 us: through_experts(): result = expert_fn(received.reshape(-1, feature))]
    dot_general x9 -> x0, matrix products: 43 us -> none  [the longest x1 11.3 us: backward_expert(): lax.dot_general(d_gate, gate_local, contract, preferred_element_type=jnp....]
    reduce_sum x8 -> x0, other arithmetic: 14.7 us -> none  [the longest x2 9.93 us: through_experts(): jnp.sum(returned.reshape(experts, SLICES, capacity, model_width).astype(j...]
    ppermute x2 -> x0, waiting for transfers between devices: 12.2 us -> none  [passed_along(): return lax.ppermute(block, axis, route)]
    broadcast_in_dim x2 -> x0, local copies, waits for them, and re-layouts: 10.1 us -> none  [through_experts(): outgoing = jnp.repeat(packed, SLICES, axis=0)]
  transfers between devices with their start and end apart: 6 -> 0, of which waited for: 5 -> 0; matrix products, arithmetic and copies ran while one was open for 15% -> 0% of each run, Pallas kernels for 0% -> 0%
where the time goes in v1:
time: 185 us
  Pallas kernels  181 us (98%)
  local copies, waits for them, and re-layouts  3.17 us (2%)
    pallas_call x1, Pallas kernels, per_device(): pl.pallas_call(kernel, out_shape=(out, out), in_specs=[hbm, vm, vm, hbm,...  181 us

profile of v1, /device:TPU:1, one launch (start us, length us, event | category | flops | bytes accessed | tf_op | source)
XLA Modules:
  0.0 185.2 jit_solution(6491627334623717280)
XLA Ops:
  0.6 181.3 %dualpipe_step.1 = (bf16[1,128,3584]{2,1,0:T(8,128)(2,1)}, bf16[1,128,3584]{2,1,0:T(8,128)(2,1)}) custom-call(bf16[1,128,3584]{2,1,0:T(8,128)(2,1)} %fin.1, s32[1,128]{1,0:T(1,128)} %bitcast.4, f32[1,128]{1,0:T(1,128)} %bitcast.5, bf16[1,128,3584]{2,1,0:T(8,128)(2,1)} %bin_.1, bf16[1,128,3584]{2,1,0:T(8,128)(2,1)} %bgrad.1, s32[1,128]{1,0:T(1,128)} %bitcast.6, ...), custom_call_target="tpu_custom_call" | custom-call | tf_op jit(solution)/shard_map/dualpipe_step/pallas_call | solution.py:397
  182.0 0.0 copy-start
  182.0 2.2 %copy.15 = bf16[1,128,3584]{2,1,0:T(8,128)(2,1)} copy(bf16[1,128,3584]{2,1,0:T(8,128)(2,1)} %get-tuple-element.4) | data formatting | bytes 1835008
  184.2 0.0 copy-done
  184.2 0.9 copy.16
Async XLA Ops:
  182.0 2.3 %copy-start = (bf16[1,128,3584]{2,1,0:T(8,128)(2,1)S(1)}, bf16[1,128,3584]{2,1,0:T(8,128)(2,1)}, u32[]{:S(2)}) copy-start(bf16[1,128,3584]{2,1,0:T(8,128)(2,1)} %get-tuple-element.5) | copy-start | bytes 2752516

commit v2 on v1

v2 whole, which is shorter than its diff:
```python
import jax
import jax.numpy as jnp
from jax import lax
from jax.experimental import pallas as pl
from jax.experimental.pallas import tpu as pltpu
from jax.sharding import PartitionSpec as P

MESH = pl.DeviceIdType.MESH
NP, NZ, NY = 8, 8, 4
T = 128
D = 3584
C = 896
W = D + C
H = 256
KC = 512
NK = D // KC
F32, BF16 = jnp.float32, jnp.bfloat16
ORDER = (4, 3, 5, 2, 6, 1, 7)
NEAR = (1, 7, 2, 6, 3, 5, 4)
FAR = (4, 3, 5, 2, 6, 1, 7, 0)
GROUPS = ((0, 2048), (2048, 2432))
LAG = 3
HALF0, HALF1, ALL = (0, 4), (4, 4), (0, 8)


def dot_nn(a, b):
    return lax.dot_general(a, b, (((1,), (0,)), ((), ())), preferred_element_type=F32)


def dot_nt(a, b):
    return lax.dot_general(a, b, (((1,), (1,)), ((), ())), preferred_element_type=F32)


def iota(shape, dim):
    return lax.broadcasted_iota(jnp.int32, shape, dim)


def slots_of(route_row, z):
    onehot = (iota((16, T), 0) == route_row).astype(F32)
    before = (iota((T, T), 0) < iota((T, T), 1)).astype(F32).astype(BF16)
    count = dot_nn(onehot.astype(BF16), before)
    rank = jnp.sum(count * onehot, axis=0, keepdims=True)
    place = jnp.zeros_like(rank)
    for n, d in enumerate(FAR):
        place = place + jnp.where(route_row == (z + d) % NZ, float(n), 0.0)
    slots = []
    for base in (route_row.astype(F32) * 16.0, place * 16.0):
        slots.append(jnp.where(rank < 15.5, base + rank, -1000.0))
        slots.append(jnp.where(rank < 15.5, -1000.0, base + rank - 16.0))
    return slots


def placing(slot_row):
    return (iota((T, T), 0).astype(F32) == slot_row).astype(F32)


def column(row):
    return jnp.transpose(jnp.broadcast_to(row, (T, T)))[:, 0:1]


def unfold(k, nb):
    m, n = iota((4 * nb, 16 * nb), 0), iota((4 * nb, 16 * nb), 1)
    return (n == (m >> 2) * 16 + (m & 3) + 4 * k).astype(F32).astype(BF16)


def fold(k, nb):
    n, m = iota((16 * nb, 4 * nb), 0), iota((16 * nb, 4 * nb), 1)
    return (n == (m >> 2) * 16 + (m & 3) + 4 * k).astype(F32).astype(BF16)


def kernel(
    fin, froute, fshare, bin_, bgrad, broute, bshare, gain, gate, up, down,
    nf, nb,
    xin, shp, meta_s, meta_r, gain_s, gain_r, send, recv, pair, extra,
    gate_o, up_o, down_o, gate_r, up_r, down_r,
    acc, hid, part_s, part_r, own, eo_b, eo_f, ret_s, ret_r, qbuf, pick, outs,
    lsem, zs, zr, ys, yr, ws, wr, ps, pr, rs, rr, xs, xr, osem,
):
    p = lax.axis_index("pipe")
    i = lax.axis_index("expert")
    z, y = i // NY, i % NY
    core = p % 2
    nxt, prv = (p + 1) % NP, (p + NP - 1) % NP
    ya = y + 1 - 2 * (y % 2)
    yb = (y + NY - 1 + 2 * (y % 2)) % NY
    yt = ya * (1 - core) + yb * core
    yw = ya * core + yb * (1 - core)

    def at_z(pp, zz):
        return (pp, zz * NY + y)

    tok = (p, z * NY + yt)
    wgt = (p, z * NY + yw)

    def remote(src, dst, s, r, device):
        return pltpu.make_async_remote_copy(
            src_ref=src, dst_ref=dst, send_sem=s, recv_sem=r, device_id=device, device_id_type=MESH
        )

    bar = pltpu.get_barrier_semaphore()

    def greet(d, _):
        pl.semaphore_signal(bar, inc=1, device_id=at_z(nxt, (z + d) % NZ), device_id_type=MESH)
        pl.semaphore_signal(bar, inc=1, device_id=at_z(prv, (z + d) % NZ), device_id_type=MESH)
        return 0

    def greet_own(d, _):
        pl.semaphore_signal(bar, inc=1, device_id=at_z(p, (z + d) % NZ), device_id_type=MESH)
        return 0

    lax.fori_loop(0, NZ, greet, 0)
    lax.fori_loop(1, NZ, greet_own, 0)
    pl.semaphore_signal(bar, inc=1, device_id=tok, device_id_type=MESH)
    pl.semaphore_signal(bar, inc=1, device_id=wgt, device_id_type=MESH)

    loads = [
        pltpu.make_async_copy(bgrad.at[0], xin.at[0], lsem.at[0]),
        pltpu.make_async_copy(bin_.at[0], xin.at[1], lsem.at[1]),
        pltpu.make_async_copy(fin.at[0], xin.at[2], lsem.at[2]),
        pltpu.make_async_copy(down.at[0], down_o, lsem.at[3]),
        pltpu.make_async_copy(gate.at[0], gate_o, lsem.at[4]),
        pltpu.make_async_copy(up.at[0], up_o, lsem.at[5]),
    ]
    for n in (2, 0, 1, 4, 5, 3):
        loads[n].start()

    def pack(j, main, ex, chunk):
        pm = placing(main).astype(BF16)
        folded = jnp.zeros((T, C), F32)
        for k in range(4):
            v = chunk(k)
            send[j, :, :, k * C:(k + 1) * C] = dot_nn(pm, v).astype(BF16).reshape(NZ, 16, C)
            folded = folded + dot_nn(placing(ex + 4.0 * k).astype(BF16), v)
        send[j, :, :, D:] = folded.astype(BF16).reshape(NZ, 16, C)

    def inv_rms(ref):
        total = jnp.zeros((T, 1), F32)
        for k in range(4):
            v = ref[:, k * C:(k + 1) * C].astype(F32)
            total = total + jnp.sum(v * v, axis=1, keepdims=True)
        return lax.rsqrt(total / D + 1e-6)

    def pack_normed(j, main, ex):
        loads[j].wait()
        r = inv_rms(xin.at[j])
        pack(j, main, ex, lambda k: (
            xin[j, :, k * C:(k + 1) * C].astype(F32) * r * gain[:, k * C:(k + 1) * C]).astype(BF16))

    def z_copy(j, d):
        return remote(send.at[j, (z + d) % NZ], recv.at[j, z], zs.at[j, d], zr.at[j, d], at_z(p, (z + d) % NZ))

    def relay_copy(j, d):
        src = (z - d + NZ) % NZ
        ref = send.at[j, src] if d == 0 else recv.at[j, src]
        return remote(ref, pair.at[j, src], ys.at[j, d], yr.at[j, d], tok)

    def relay(j, ds):
        for d in ds:
            if d:
                z_copy(j, d).wait_recv()
            relay_copy(j, d).start()

    def keep(j):
        return pltpu.make_async_copy(send.at[j, z], recv.at[j, z], lsem.at[6 + j])

    def z_send(j):
        for d in ORDER:
            z_copy(j, d).start()
        keep(j).start()

    weight_copies = [
        remote(gate.at[0], gate_r, ws.at[0], wr.at[0], wgt),
        remote(up.at[0], up_r, ws.at[1], wr.at[1], wgt),
        remote(down.at[0], down_r, ws.at[2], wr.at[2], wgt),
    ]

    fmain, fextra, ftake, ftake_ex = slots_of(froute[...], z)
    pack_normed(2, fmain, fextra)
    pl.semaphore_wait(bar, 25)
    for c in weight_copies:
        c.start()
    z_send(2)

    bmain, bextra, btake, btake_ex = slots_of(broute[...], z)
    loads[0].wait()
    share_col = column(bshare[...])
    pack(0, bmain, bextra, lambda k: (share_col * xin[0, :, k * C:(k + 1) * C].astype(F32)).astype(BF16))
    z_send(0)
    pack_normed(1, bmain, bextra)
    z_send(1)

    def rows(*parts):
        return jnp.concatenate(list(parts) + [jnp.zeros((8 - len(parts), T), F32)], axis=0)

    meta_s[0] = rows(btake, btake_ex)
    meta_s[1] = rows(ftake, ftake_ex, fshare[...])
    gain_s[...] = jnp.broadcast_to(gain[...], (8, D))
    down_pipe, up_pipe = (prv, i), (nxt, i)
    ship = [
        remote(meta_s.at[0], meta_r.at[0], xs.at[0], xr.at[0], down_pipe),
        remote(gain_s, gain_r, xs.at[1], xr.at[1], down_pipe),
        remote(xin.at[0], shp.at[0], xs.at[2], xr.at[2], down_pipe),
        remote(xin.at[1], shp.at[1], xs.at[3], xr.at[3], down_pipe),
        remote(meta_s.at[1], meta_r.at[1], xs.at[4], xr.at[4], up_pipe),
        remote(xin.at[2], shp.at[2], xs.at[5], xr.at[5], up_pipe),
    ]
    for c in ship:
        c.start()

    PAIR, OWN = 0, 160

    def source(n):
        return (z - FAR[n] + NZ) % NZ

    def first(j, part, half, mats):
        src = recv if part else pair
        pos, nb = half
        e0 = (32 if part else 0) + 4 * pos

        def blocks(ds):
            return [src[j, source(n), :, ds] for n in range(pos, pos + nb)]

        folded = jnp.concatenate(blocks(slice(D, W)), axis=0)
        for k in range(4):
            extra[j, e0:e0 + 4 * nb, k * C:(k + 1) * C] = dot_nn(unfold(k, nb), folded).astype(BF16)
        at = pl.ds(part + 16 * pos, 16 * nb)
        at_ex = pl.ds(part + 128 + 4 * pos, 4 * nb)
        for m, _, _ in mats:
            acc[m, at] = jnp.zeros((16 * nb, H), F32)
            acc[m, at_ex] = jnp.zeros((4 * nb, H), F32)

        def step(n, _):
            ds = pl.ds(pl.multiple_of(n * KC, KC), KC)
            v = jnp.concatenate(blocks(ds) + [extra[j, e0:e0 + 4 * nb, ds]], axis=0)
            for m, w, transposed in mats:
                o = dot_nt(v, w[:, ds]) if transposed else dot_nn(v, w[ds, :])
                acc[m, at] += o[:16 * nb]
                acc[m, at_ex] += o[16 * nb:]
            return 0

        lax.fori_loop(0, NK, step, 0)

    def have_pair(j, half):
        for n in range(half[0], half[0] + half[1]):
            relay_copy(j, FAR[n]).wait_recv()

    gate_up = [(2, gate_o, False), (3, gate_r, False), (4, up_o, False), (5, up_r, False)]
    downs = [(0, down_o, True), (1, down_r, True)]

    def act(fn, part, half):
        pos, nb = half

        def step(n, _):
            fn(pl.ds(pl.multiple_of(part + 16 * pos + n * 32, 32), 32))
            return 0

        lax.fori_loop(0, nb // 2, step, 0)
        fn(pl.ds(part + 128 + 4 * pos, 4 * nb))

    def act_fwd(ds):
        for s in range(2):
            pg, pu = acc[2 + s, ds], acc[4 + s, ds]
            hid[s, ds] = (pg * jax.nn.sigmoid(pg) * pu).astype(BF16)

    def act_back(ds):
        for s in range(2):
            dh, pg, pu = acc[s, ds], acc[2 + s, ds], acc[4 + s, ds]
            sg = jax.nn.sigmoid(pg)
            hid[2 + s, ds] = (dh * pu * sg * (1.0 + pg * (1.0 - sg))).astype(BF16)
            hid[4 + s, ds] = (dh * pg * sg).astype(BF16)

    def hidden(n, part, half):
        pos, nb = half
        return jnp.concatenate(
            [hid[n, pl.ds(part + 16 * pos, 16 * nb)], hid[n, pl.ds(part + 128 + 4 * pos, 4 * nb)]], axis=0)

    def out_rows(b, part, half, ds):
        h = [hidden(n, part, half) for n in ((2, 3, 4, 5) if b == 0 else (0, 1))]
        if b == 1:
            return dot_nn(h[0], down_o[:, ds]) + dot_nn(h[1], down_r[:, ds])
        return (dot_nt(h[0], gate_o[ds, :]) + dot_nt(h[1], gate_r[ds, :])
                + dot_nt(h[2], up_o[ds, :]) + dot_nt(h[3], up_r[ds, :]))

    def cols(n):
        return pl.ds(n * KC, KC) if isinstance(n, int) else pl.ds(pl.multiple_of(n * KC, KC), KC)

    def part_copy(b, half, n):
        ds = pl.ds(D, C) if isinstance(n, int) and n == NK else cols(n)
        at, h = pl.ds(*half), half[0] // 4
        return remote(part_s.at[b, at, :, ds], part_r.at[b, at, :, ds], ps.at[b, h, n], pr.at[b, h, n], tok)

    def fold_extra(dst, b, half):
        pos, nb = half
        folded = jnp.zeros((16 * nb, C), F32)
        for k in range(4):
            folded = folded + dot_nn(fold(k, nb), eo_b[4 * pos:4 * (pos + nb), k * C:(k + 1) * C])
        dst[b, pos:pos + nb, :, D:] = folded.astype(BF16).reshape(nb, 16, C)

    def theirs(b, half, n):
        pos, nb = half
        ds = cols(n)
        o = out_rows(b, PAIR, half, ds).astype(BF16)
        part_s[b, pos:pos + nb, :, ds] = o[:16 * nb].reshape(nb, 16, KC)
        eo_b[4 * pos:4 * (pos + nb), ds] = o[16 * nb:]
        part_copy(b, half, n).start()

    def theirs_extra(b, half):
        fold_extra(part_s, b, half)
        part_copy(b, half, NK).start()

    def ours(b, half, n):
        pos, nb = half
        ds = cols(n)
        o = out_rows(b, OWN, half, ds)
        own[16 * pos:16 * (pos + nb), ds] = o[:16 * nb]
        eo_f[4 * pos:4 * (pos + nb), ds] = o[16 * nb:]

    def ret_copy(b, g, n):
        ds = pl.ds(*GROUPS[g])
        return remote(ret_s.at[b, n, :, ds], ret_r.at[b, n, :, ds], rs.at[b, g, n], rr.at[b, g, n],
                      at_z(prv if b == 0 else nxt, source(n)))

    def ret_send(b, half, g):
        for n in range(half[0], half[0] + half[1]):
            ret_copy(b, g, n).start()

    def add(b, half, n):
        pos, nb = half
        ds = cols(n)
        part_copy(b, half, n).wait_recv()
        o = own[16 * pos:16 * (pos + nb), ds] + part_r[b, pos:pos + nb, :, ds].reshape(16 * nb, KC).astype(F32)
        ret_s[b, pos:pos + nb, :, ds] = o.astype(BF16).reshape(nb, 16, KC)
        if n == 3:
            ret_send(b, half, 0)

    def add_extra(b, half):
        pos, nb = half
        part_copy(b, half, NK).wait_recv()
        folded = part_r[b, pos:pos + nb, :, D:].reshape(16 * nb, C)
        for k in range(4):
            ks = slice(k * C, (k + 1) * C)
            at = slice(4 * pos, 4 * (pos + nb))
            eo_b[at, ks] = (eo_f[at, ks] + dot_nn(unfold(k, nb), folded)).astype(BF16)
        fold_extra(ret_s, b, half)
        ret_send(b, half, 1)

    def repeat(fn, b, half):
        def step(n, _):
            fn(b, half, n)
            return 0

        lax.fori_loop(0, NK, step, 0)

    def add_all(b, half):
        for n in range(NK):
            add(b, half, n)
        add_extra(b, half)

    def back_end(half):
        for n in range(NK + LAG):
            if n < NK:
                theirs(0, half, n)
            if n == NK - 1:
                theirs_extra(0, half)
            if n >= LAG:
                ours(0, half, n - LAG)
                add(0, half, n - LAG)
        add_extra(0, half)

    relay(2, (0,) + NEAR)
    keep(2).wait()
    loads[4].wait()
    loads[5].wait()
    loads[3].wait()
    weight_copies[0].wait_recv()
    weight_copies[1].wait_recv()
    first(2, OWN, ALL, gate_up)
    act(act_fwd, OWN, ALL)
    have_pair(2, ALL)
    first(2, PAIR, ALL, gate_up)
    act(act_fwd, PAIR, ALL)
    weight_copies[2].wait_recv()
    repeat(theirs, 1, ALL)
    theirs_extra(1, ALL)
    relay(0, FAR[:4])
    relay(1, FAR[:4])
    relay(0, FAR[4:])
    repeat(ours, 1, ALL)
    for d in NEAR:
        if d in FAR[4:]:
            z_copy(1, d).wait_recv()
    keep(0).wait()
    first(0, OWN, ALL, downs)
    keep(1).wait()
    first(1, OWN, ALL, gate_up)
    act(act_back, OWN, ALL)
    add_all(1, ALL)
    have_pair(0, HALF0)
    first(0, PAIR, HALF0, downs)
    have_pair(1, HALF0)
    first(1, PAIR, HALF0, gate_up)
    act(act_back, PAIR, HALF0)
    repeat(theirs, 0, HALF0)
    theirs_extra(0, HALF0)
    for d in FAR[4:]:
        relay_copy(1, d).start()
    repeat(ours, 0, HALF0)
    have_pair(0, HALF1)
    first(0, PAIR, HALF1, downs)
    add_all(0, HALF0)
    have_pair(1, HALF1)
    first(1, PAIR, HALF1, gate_up)
    act(act_back, PAIR, HALF1)
    back_end(HALF1)

    for c in ship:
        c.wait()
    for b in range(2):
        main, ex = meta_r[b, 0:1, :], meta_r[b, 1:2, :]
        pick[b, 0] = jnp.transpose(placing(main)).astype(BF16)
        for k in range(4):
            pick[b, 1 + k] = jnp.transpose(placing(ex + 4.0 * k)).astype(BF16)

    def take(b, half, k):
        pos, nb = half
        at = slice(16 * pos, 16 * (pos + nb))
        main = ret_r[b, pos:pos + nb, :, k * C:(k + 1) * C].reshape(16 * nb, C)
        return dot_nn(pick[b, 0][:, at], main) + dot_nn(
            pick[b, 1 + k][:, at], ret_r[b, pos:pos + nb, :, D:].reshape(16 * nb, C))

    def have_ret(b, half):
        for g in range(2):
            for n in range(half[0], half[0] + half[1]):
                ret_copy(b, g, n).wait_recv()

    share_fwd = column(meta_r[1, 2:3, :])
    r = inv_rms(shp.at[1])
    have_ret(1, ALL)
    for k in range(4):
        ks = slice(k * C, (k + 1) * C)
        outs[1, :, ks] = (shp[2, :, ks].astype(F32) + share_fwd * take(1, ALL, k)).astype(BF16)
    out_f = pltpu.make_async_copy(outs.at[1], nf.at[0], osem.at[0])
    out_f.start()

    have_ret(0, HALF0)
    for k in range(4):
        qbuf[:, k * C:(k + 1) * C] = take(0, HALF0, k)
    for j in range(3):
        for d in range(NZ):
            if d:
                z_copy(j, d).wait_send()
            relay_copy(j, d).wait_send()
        weight_copies[j].wait_send()
    for b, half in ((1, ALL), (0, HALF0), (0, HALF1)):
        for n in range(NK + 1):
            part_copy(b, half, n).wait_send()
    for b in range(2):
        for g in range(2):
            for n in range(NZ):
                ret_copy(b, g, n).wait_send()

    have_ret(0, HALF1)
    total = jnp.zeros((T, 1), F32)
    for k in range(4):
        ks = slice(k * C, (k + 1) * C)
        q = gain_r[0:1, ks] * (qbuf[:, ks] + take(0, HALF1, k))
        qbuf[:, ks] = q
        total = total + jnp.sum(shp[1, :, ks].astype(F32) * q, axis=1, keepdims=True)
    coef = r * r * r * (total / D)
    out_b = []
    for k in range(4):
        ks = slice(k * C, (k + 1) * C)
        outs[0, :, ks] = (
            shp[0, :, ks].astype(F32) + (r * qbuf[:, ks] - shp[1, :, ks].astype(F32) * coef)).astype(BF16)
        out_b.append(pltpu.make_async_copy(outs.at[0, :, pl.ds(k * C, C)], nb.at[0, :, pl.ds(k * C, C)], osem.at[1 + k]))
        out_b[-1].start()

    out_f.wait()
    for c in out_b:
        c.wait()


def per_device(fin, froute, fshare, bin_, bgrad, broute, bshare, gain, gate, up, down):
    vm = pl.BlockSpec(memory_space=pltpu.VMEM)
    hbm = pl.BlockSpec(memory_space=pl.ANY)
    dma = pltpu.SemaphoreType.DMA
    out = jax.ShapeDtypeStruct((1, T, D), BF16)
    v = pltpu.VMEM
    return pl.pallas_call(
        kernel,
        out_shape=(out, out),
        in_specs=[hbm, vm, vm, hbm, hbm, vm, vm, vm, hbm, hbm, hbm],
        out_specs=(hbm, hbm),
        scratch_shapes=[
            v((3, T, D), BF16), v((3, T, D), BF16), v((2, 8, T), F32), v((2, 8, T), F32),
            v((8, D), F32), v((8, D), F32),
            v((3, NZ, 16, W), BF16), v((3, NZ, 16, W), BF16), v((3, NZ, 16, W), BF16), v((3, 64, D), BF16),
            v((D, H), BF16), v((D, H), BF16), v((H, D), BF16),
            v((D, H), BF16), v((D, H), BF16), v((H, D), BF16),
            v((6, 320, H), F32), v((6, 320, H), BF16),
            v((2, NZ, 16, W), BF16), v((2, NZ, 16, W), BF16),
            v((T, D), F32), v((32, D), BF16), v((32, D), F32),
            v((2, NZ, 16, W), BF16), v((2, NZ, 16, W), BF16), v((T, D), F32),
            v((2, 5, T, T), BF16), v((2, T, D), BF16),
            dma((9,)), dma((3, NZ)), dma((3, NZ)), dma((3, NZ)), dma((3, NZ)),
            dma((3,)), dma((3,)), dma((2, 2, NK + 1)), dma((2, 2, NK + 1)),
            dma((2, 2, NZ)), dma((2, 2, NZ)), dma((6,)), dma((6,)), dma((5,)),
        ],
        compiler_params=pltpu.CompilerParams(
            collective_id=1, has_side_effects=True, vmem_limit_bytes=60 << 20
        ),
        name="dualpipe_step",
    )(
        fin, froute.reshape(1, T), fshare.reshape(1, T), bin_, bgrad, broute.reshape(1, T),
        bshare.reshape(1, T), gain, gate, up, down,
    )


def solution(mesh):
    spec = P("pipe", "expert", None)
    return jax.shard_map(
        per_device,
        mesh=mesh,
        in_specs=(
            spec, spec, spec, spec, spec, spec, spec,
            P("pipe", None), P("pipe", None, "expert"), P("pipe", None, "expert"), P("pipe", "expert", None),
        ),
        out_specs=(spec, spec),
        check_vma=False,
    )
```

time: 185 us -> 160 us (0.86)
  Pallas kernels: 181 us -> 156 us
    pallas_call x1, Pallas kernels: 181 us -> 156 us  [per_device(): pl.pallas_call(kernel, out_shape=(out, out), in_specs=[hbm, vm, vm, hbm,...]
where the time goes in v2:
time: 160 us; the launch traced here: 159 us
  Pallas kernels  156 us (98%)
  local copies, waits for them, and re-layouts  3.17 us (2%)
    pallas_call x1, Pallas kernels, per_device(): pl.pallas_call(kernel, out_shape=(out, out), in_specs=[hbm, vm, vm, hbm,...  156 us

profile of v2, /device:TPU:1, one launch (start us, length us, event | category | flops | bytes accessed | tf_op | source)
XLA Modules:
  0.0 159.5 jit_solution(12943299976229193478)
XLA Ops:
  0.6 155.6 %dualpipe_step.1 = (bf16[1,128,3584]{2,1,0:T(8,128)(2,1)}, bf16[1,128,3584]{2,1,0:T(8,128)(2,1)}) custom-call(bf16[1,128,3584]{2,1,0:T(8,128)(2,1)} %fin.1, s32[1,128]{1,0:T(1,128)} %bitcast.4, f32[1,128]{1,0:T(1,128)} %bitcast.5, bf16[1,128,3584]{2,1,0:T(8,128)(2,1)} %bin_.1, bf16[1,128,3584]{2,1,0:T(8,128)(2,1)} %bgrad.1, s32[1,128]{1,0:T(1,128)} %bitcast.6, ...), custom_call_target="tpu_custom_call" | custom-call | tf_op jit(solution)/shard_map/dualpipe_step/pallas_call | solution.py:489
  156.3 0.0 copy-start
  156.3 2.2 %copy.15 = bf16[1,128,3584]{2,1,0:T(8,128)(2,1)} copy(bf16[1,128,3584]{2,1,0:T(8,128)(2,1)} %get-tuple-element.4) | data formatting | bytes 1835008
  158.5 0.0 copy-done
  158.5 0.9 copy.16
Async XLA Ops:
  156.3 2.3 %copy-start = (bf16[1,128,3584]{2,1,0:T(8,128)(2,1)S(1)}, bf16[1,128,3584]{2,1,0:T(8,128)(2,1)}, u32[]{:S(2)}) copy-start(bf16[1,128,3584]{2,1,0:T(8,128)(2,1)} %get-tuple-element.5) | copy-start | bytes 2752516

commit v3 on v2

v3 whole, which is shorter than its diff:
```python
import jax
import jax.numpy as jnp
from jax import lax
from jax.experimental import pallas as pl
from jax.experimental.pallas import tpu as pltpu
from jax.sharding import PartitionSpec as P

MESH = pl.DeviceIdType.MESH
NP, NZ, NY = 8, 8, 4
T = 128
D = 3584
C = 896
W = D + C
H = 256
KC = 512
NK = D // KC
F32, BF16 = jnp.float32, jnp.bfloat16
ORDER = (4, 3, 5, 2, 6, 1, 7)
NEAR = (1, 7, 2, 6, 3, 5, 4)
FAR = (4, 3, 5, 2, 6, 1, 7, 0)
COLS = ((0, 1024), (1024, 1024), (2048, 1024), (3072, 1408))
GROUP = ((0, 3), (3, 3), (6, 2))
NG = len(GROUP)
ALL = tuple(range(NG))
PART = T + 16 * NG


def span(gs):
    return GROUP[gs[0]][0], sum(GROUP[g][1] for g in gs)


def dot_nn(a, b):
    return lax.dot_general(a, b, (((1,), (0,)), ((), ())), preferred_element_type=F32)


def dot_nt(a, b):
    return lax.dot_general(a, b, (((1,), (1,)), ((), ())), preferred_element_type=F32)


def iota(shape, dim):
    return lax.broadcasted_iota(jnp.int32, shape, dim)


def slots_of(route_row, z):
    onehot = (iota((16, T), 0) == route_row).astype(F32)
    before = (iota((T, T), 0) < iota((T, T), 1)).astype(F32).astype(BF16)
    count = dot_nn(onehot.astype(BF16), before)
    rank = jnp.sum(count * onehot, axis=0, keepdims=True)
    place = jnp.zeros_like(rank)
    for n, d in enumerate(FAR):
        place = place + jnp.where(route_row == (z + d) % NZ, float(n), 0.0)
    slots = []
    for base in (route_row.astype(F32) * 16.0, place * 16.0):
        slots.append(jnp.where(rank < 15.5, base + rank, -1000.0))
        slots.append(jnp.where(rank < 15.5, -1000.0, base + rank - 16.0))
    return slots


def placing(slot_row):
    return (iota((T, T), 0).astype(F32) == slot_row).astype(F32)


def column(row):
    return jnp.transpose(jnp.broadcast_to(row, (T, T)))[:, 0:1]


def unfold(k, nb):
    m, n = iota((16, 16 * nb), 0), iota((16, 16 * nb), 1)
    return (n == (m >> 2) * 16 + (m & 3) + 4 * k).astype(F32).astype(BF16)


def fold(k, nb):
    n, m = iota((16 * nb, 16), 0), iota((16 * nb, 16), 1)
    return (n == (m >> 2) * 16 + (m & 3) + 4 * k).astype(F32).astype(BF16)


def kernel(
    fin, froute, fshare, bin_, bgrad, broute, bshare, gain, gate, up, down,
    nf, nb,
    xin, shp, meta_s, meta_r, gain_s, gain_r, send, recv, pair, extra,
    gate_o, up_o, down_o, gate_r, up_r, down_r,
    acc, hid, part_s, part_r, own, eo_b, eo_f, ret_s, ret_r, qbuf, pick0, pick1, outs,
    lsem, zs, zr, zrf, ys, yr, ws, wr, ps, pr, rs, rr, xs, xr, osem,
):
    p = lax.axis_index("pipe")
    i = lax.axis_index("expert")
    z, y = i // NY, i % NY
    core = p % 2
    nxt, prv = (p + 1) % NP, (p + NP - 1) % NP
    ya = y + 1 - 2 * (y % 2)
    yb = (y + NY - 1 + 2 * (y % 2)) % NY
    yt = ya * (1 - core) + yb * core
    yw = ya * core + yb * (1 - core)

    def at_z(pp, zz):
        return (pp, zz * NY + y)

    tok = (p, z * NY + yt)
    wgt = (p, z * NY + yw)

    def remote(src, dst, s, r, device):
        return pltpu.make_async_remote_copy(
            src_ref=src, dst_ref=dst, send_sem=s, recv_sem=r, device_id=device, device_id_type=MESH
        )

    loads = [
        pltpu.make_async_copy(bgrad.at[0], xin.at[0], lsem.at[0]),
        pltpu.make_async_copy(bin_.at[0], xin.at[1], lsem.at[1]),
        pltpu.make_async_copy(fin.at[0], xin.at[2], lsem.at[2]),
        pltpu.make_async_copy(down.at[0], down_o, lsem.at[3]),
        pltpu.make_async_copy(gate.at[0], gate_o, lsem.at[4]),
        pltpu.make_async_copy(up.at[0], up_o, lsem.at[5]),
    ]
    for n in (2, 0, 1, 4, 5, 3):
        loads[n].start()

    bar = pltpu.get_barrier_semaphore()

    def greet(d, _):
        pl.semaphore_signal(bar, inc=1, device_id=at_z(nxt, (z + d) % NZ), device_id_type=MESH)
        pl.semaphore_signal(bar, inc=1, device_id=at_z(prv, (z + d) % NZ), device_id_type=MESH)
        return 0

    def greet_own(d, _):
        pl.semaphore_signal(bar, inc=1, device_id=at_z(p, (z + d) % NZ), device_id_type=MESH)
        return 0

    lax.fori_loop(0, NZ, greet, 0)
    lax.fori_loop(1, NZ, greet_own, 0)
    pl.semaphore_signal(bar, inc=1, device_id=tok, device_id_type=MESH)
    pl.semaphore_signal(bar, inc=1, device_id=wgt, device_id_type=MESH)

    def pack(j, main, ex, chunk):
        pm = placing(main).astype(BF16)
        folded = jnp.zeros((T, C), F32)
        for k in range(4):
            v = chunk(k)
            send[j, :, :, k * C:(k + 1) * C] = dot_nn(pm, v).astype(BF16).reshape(NZ, 16, C)
            folded = folded + dot_nn(placing(ex + 4.0 * k).astype(BF16), v)
        send[j, :, :, D:] = folded.astype(BF16).reshape(NZ, 16, C)

    def inv_rms(ref):
        total = jnp.zeros((T, 1), F32)
        for k in range(4):
            v = ref[:, k * C:(k + 1) * C].astype(F32)
            total = total + jnp.sum(v * v, axis=1, keepdims=True)
        return lax.rsqrt(total / D + 1e-6)

    def pack_normed(j, main, ex):
        loads[j].wait()
        r = inv_rms(xin.at[j])
        pack(j, main, ex, lambda k: (
            xin[j, :, k * C:(k + 1) * C].astype(F32) * r * gain[:, k * C:(k + 1) * C]).astype(BF16))

    def z_copy(j, d):
        return remote(send.at[j, (z + d) % NZ], recv.at[j, z], zs.at[j],
                      zrf.at[d] if j == 2 else zr.at[j], at_z(p, (z + d) % NZ))

    def z_all(j):
        return remote(send.at[j, pl.ds(0, 7)], recv.at[j, pl.ds(0, 7)], zs.at[j], zr.at[j % 2], tok)

    def relay_copy(j, d):
        src = (z - d + NZ) % NZ
        ref = send.at[j, src] if d == 0 else recv.at[j, src]
        g = 0
        if j < 2:
            g = [d in FAR[lo:lo + nb] for lo, nb in GROUP].index(True)
        return remote(ref, pair.at[j, src], ys.at[j], yr.at[j, g], tok)

    def relay_all(j, nb, g):
        return remote(recv.at[j, pl.ds(0, nb)], pair.at[j, pl.ds(0, nb)], ys.at[j], yr.at[j, g], tok)

    def relay(j, ds):
        for d in ds:
            relay_copy(j, d).start()

    def keep(j):
        return pltpu.make_async_copy(send.at[j, z], recv.at[j, z], lsem.at[6 + j])

    def z_send(j):
        for d in ORDER:
            z_copy(j, d).start()
        keep(j).start()

    weight_copies = [
        remote(gate.at[0], gate_r, ws.at[0], wr.at[0], wgt),
        remote(up.at[0], up_r, ws.at[1], wr.at[1], wgt),
        remote(down.at[0], down_r, ws.at[2], wr.at[2], wgt),
    ]

    pl.semaphore_wait(bar, 25)
    for c in weight_copies:
        c.start()
    fmain, fextra, ftake, ftake_ex = slots_of(froute[...], z)
    pack_normed(2, fmain, fextra)
    z_send(2)

    bmain, bextra, btake, btake_ex = slots_of(broute[...], z)
    loads[0].wait()
    share_col = column(bshare[...])
    pack(0, bmain, bextra, lambda k: (share_col * xin[0, :, k * C:(k + 1) * C].astype(F32)).astype(BF16))
    z_send(0)
    pack_normed(1, bmain, bextra)
    z_send(1)

    def rows(*parts):
        return jnp.concatenate(list(parts) + [jnp.zeros((8 - len(parts), T), F32)], axis=0)

    meta_s[0] = rows(btake, btake_ex)
    meta_s[1] = rows(ftake, ftake_ex, fshare[...])
    gain_s[...] = jnp.broadcast_to(gain[...], (8, D))
    down_pipe, up_pipe = (prv, i), (nxt, i)
    ship = [
        remote(meta_s.at[0], meta_r.at[0], xs.at[0], xr.at[0], down_pipe),
        remote(gain_s, gain_r, xs.at[1], xr.at[1], down_pipe),
        remote(xin.at[0], shp.at[0], xs.at[2], xr.at[2], down_pipe),
        remote(xin.at[1], shp.at[1], xs.at[3], xr.at[3], down_pipe),
        remote(meta_s.at[1], meta_r.at[1], xs.at[4], xr.at[4], up_pipe),
        remote(xin.at[2], shp.at[2], xs.at[5], xr.at[5], up_pipe),
    ]
    for c in ship:
        c.start()

    PAIR, OWN = 0, PART

    def source(n):
        return (z - FAR[n] + NZ) % NZ

    def row_sets(part, gs):
        pos, nb = span(gs)
        return pl.ds(part + 16 * pos, 16 * nb), pl.ds(part + T + 16 * gs[0], 16 * len(gs))

    def first(j, part, gs, mats, unfolded=False):
        src = recv if part else pair
        pos, nb = span(gs)
        e0 = 16 * NG if part else 0
        es = slice(e0 + 16 * gs[0], e0 + 16 * (gs[-1] + 1))

        def blocks(lo, n, ds):
            return [src[j, source(m), :, ds] for m in range(lo, lo + n)]

        if not unfolded:
            for g in gs:
                folded = jnp.concatenate(blocks(*GROUP[g], slice(D, W)), axis=0)
                for k in range(4):
                    extra[j, e0 + 16 * g:e0 + 16 * (g + 1), k * C:(k + 1) * C] = dot_nn(
                        unfold(k, GROUP[g][1]), folded).astype(BF16)
        at, at_ex = row_sets(part, gs)
        for m, _, _ in mats:
            acc[m, at] = jnp.zeros((16 * nb, H), F32)
            acc[m, at_ex] = jnp.zeros((16 * len(gs), H), F32)

        def step(n, _):
            ds = pl.ds(pl.multiple_of(n * KC, KC), KC)
            v = jnp.concatenate(blocks(pos, nb, ds) + [extra[j, es, ds]], axis=0)
            for m, w, transposed in mats:
                o = dot_nt(v, w[:, ds]) if transposed else dot_nn(v, w[ds, :])
                acc[m, at] += o[:16 * nb]
                acc[m, at_ex] += o[16 * nb:]
            return 0

        lax.fori_loop(0, NK, step, 0)

    def have_pair(j, gs):
        relay_all(j, span(gs)[1], gs[0]).wait_recv()

    gate_up = [(2, gate_o, False), (3, gate_r, False), (4, up_o, False), (5, up_r, False)]
    downs = [(0, down_o, True), (1, down_r, True)]

    def act(fn, part, gs):
        at, at_ex = row_sets(part, gs)

        def step(n, _):
            fn(pl.ds(pl.multiple_of(at.start + n * 16, 16), 16))
            return 0

        lax.fori_loop(0, at.size // 16, step, 0)
        fn(at_ex)

    def act_fwd(ds):
        for s in range(2):
            pg, pu = acc[2 + s, ds], acc[4 + s, ds]
            hid[s, ds] = (pg * jax.nn.sigmoid(pg) * pu).astype(BF16)

    def act_back(ds):
        for s in range(2):
            dh, pg, pu = acc[s, ds], acc[2 + s, ds], acc[4 + s, ds]
            sg = jax.nn.sigmoid(pg)
            hid[2 + s, ds] = (dh * pu * sg * (1.0 + pg * (1.0 - sg))).astype(BF16)
            hid[4 + s, ds] = (dh * pg * sg).astype(BF16)

    def out_rows(b, part, gs, ds):
        at, at_ex = row_sets(part, gs)
        h = [jnp.concatenate([hid[n, at], hid[n, at_ex]], axis=0) for n in ((2, 3, 4, 5) if b == 0 else (0, 1))]
        if b == 1:
            return dot_nn(h[0], down_o[:, ds]) + dot_nn(h[1], down_r[:, ds])
        return (dot_nt(h[0], gate_o[ds, :]) + dot_nt(h[1], gate_r[ds, :])
                + dot_nt(h[2], up_o[ds, :]) + dot_nt(h[3], up_r[ds, :]))

    def cols(n):
        return pl.ds(n * KC, KC) if isinstance(n, int) else pl.ds(pl.multiple_of(n * KC, KC), KC)

    def part_copy(b, gs, n):
        ds = pl.ds(D, C) if isinstance(n, int) and n == NK else cols(n)
        at, h = pl.ds(*span(gs)), 0 if b else 1 + gs[0]
        return remote(part_s.at[b, at, :, ds], part_r.at[b, at, :, ds], ps.at[b], pr.at[h, n], tok)

    def fold_extra(dst, b, gs):
        for g in gs:
            pos, nb = GROUP[g]
            folded = jnp.zeros((16 * nb, C), F32)
            for k in range(4):
                folded = folded + dot_nn(fold(k, nb), eo_b[16 * g:16 * (g + 1), k * C:(k + 1) * C])
            dst[b, pos:pos + nb, :, D:] = folded.astype(BF16).reshape(nb, 16, C)

    def theirs(b, gs, n):
        pos, nb = span(gs)
        ds = cols(n)
        o = out_rows(b, PAIR, gs, ds).astype(BF16)
        part_s[b, pos:pos + nb, :, ds] = o[:16 * nb].reshape(nb, 16, KC)
        eo_b[16 * gs[0]:16 * (gs[-1] + 1), ds] = o[16 * nb:]
        part_copy(b, gs, n).start()

    def theirs_extra(b, gs):
        fold_extra(part_s, b, gs)
        part_copy(b, gs, NK).start()

    def ours(b, gs, n):
        pos, nb = span(gs)
        ds = cols(n)
        o = out_rows(b, OWN, gs, ds)
        own[b, 16 * pos:16 * (pos + nb), ds] = o[:16 * nb]
        eo_f[b, 16 * gs[0]:16 * (gs[-1] + 1), ds] = o[16 * nb:]

    def ret_copy(b, g, n):
        ds = pl.ds(*COLS[g])
        return remote(ret_s.at[b, n, :, ds], ret_r.at[b, n, :, ds], rs.at[b],
                      rr.at[2 if b else n // GROUP[-1][0]], at_z(prv if b == 0 else nxt, source(n)))

    def ret_all(b, nb, h):
        at = pl.ds(0, nb)
        return remote(ret_s.at[b, at], ret_r.at[b, at], rs.at[b], rr.at[h], at_z(prv if b == 0 else nxt, z))

    def ret_send(b, gs, g):
        pos, nb = span(gs)
        for n in range(pos, pos + nb):
            ret_copy(b, g, n).start()

    def add(b, gs, n):
        pos, nb = span(gs)
        ds = cols(n)
        part_copy(b, gs, n).wait_recv()
        o = own[b, 16 * pos:16 * (pos + nb), ds] + part_r[b, pos:pos + nb, :, ds].reshape(16 * nb, KC).astype(F32)
        ret_s[b, pos:pos + nb, :, ds] = o.astype(BF16).reshape(nb, 16, KC)
        if n % 2 == 1:
            ret_send(b, gs, n // 2)

    def add_extra(b, gs):
        part_copy(b, gs, NK).wait_recv()
        for g in gs:
            pos, nb = GROUP[g]
            at = slice(16 * g, 16 * (g + 1))
            folded = part_r[b, pos:pos + nb, :, D:].reshape(16 * nb, C)
            for k in range(4):
                ks = slice(k * C, (k + 1) * C)
                eo_b[at, ks] = (eo_f[b, at, ks] + dot_nn(unfold(k, nb), folded)).astype(BF16)
        fold_extra(ret_s, b, gs)
        ret_send(b, gs, 3)

    def repeat(fn, b, gs):
        def step(n, _):
            fn(b, gs, n)
            return 0

        lax.fori_loop(0, NK, step, 0)

    def grad_rows(g):
        have_pair(0, (g,))
        first(0, PAIR, (g,), downs)

    def gate_rows(g):
        first(1, PAIR, (g,), gate_up)
        act(act_back, PAIR, (g,))

    def names(g):
        return FAR[GROUP[g][0]:GROUP[g][0] + GROUP[g][1]]

    early = span((0, 1))[1]

    def make_picks():
        for c in ship:
            c.wait()
        for b in range(2):
            main = jnp.transpose(placing(meta_r[b, 0:1, :])).astype(BF16)
            for k in range(4):
                ex = jnp.transpose(placing(meta_r[b, 1:2, :] + 4.0 * k)).astype(BF16)
                pick0[b, k] = jnp.concatenate([main[:, :16 * early], ex[:, :16 * early]], axis=1)
                pick1[b, k] = jnp.concatenate([main[:, 16 * early:], ex[:, 16 * early:]], axis=1)

    for d in (0,) + NEAR:
        if d:
            z_copy(2, d).wait_recv()
        relay(2, (d,))
    keep(2).wait()
    loads[4].wait()
    loads[5].wait()
    loads[3].wait()
    weight_copies[0].wait_recv()
    weight_copies[1].wait_recv()
    first(2, OWN, ALL, gate_up)
    act(act_fwd, OWN, ALL)
    have_pair(2, ALL)
    first(2, PAIR, ALL, gate_up)
    act(act_fwd, PAIR, ALL)
    z_all(0).wait_recv()
    keep(0).wait()
    first(0, OWN, ALL, downs[:1])
    weight_copies[2].wait_recv()
    repeat(theirs, 1, ALL)
    theirs_extra(1, ALL)
    for n in range(2):
        ours(1, ALL, n)
        add(1, ALL, n)
    relay(0, names(0))
    z_all(1).wait_recv()
    relay(1, names(0))
    for n in range(2, 4):
        ours(1, ALL, n)
        add(1, ALL, n)
    first(0, OWN, ALL, downs[1:], True)
    for n in range(4, 6):
        ours(1, ALL, n)
        add(1, ALL, n)
    relay(0, names(1))
    keep(1).wait()
    first(1, OWN, ALL, gate_up)
    ours(1, ALL, 6)
    add(1, ALL, 6)
    add_extra(1, ALL)
    act(act_back, OWN, ALL)
    repeat(ours, 0, ALL)
    grad_rows(0)
    have_pair(1, (0,))
    gate_rows(0)
    repeat(theirs, 0, (0,))
    theirs_extra(0, (0,))
    relay(1, names(1))
    relay(0, names(2))
    relay(1, names(2))
    add(0, (0,), 0)
    add(0, (0,), 1)
    grad_rows(1)
    for n in range(2, NK):
        add(0, (0,), n)
    add_extra(0, (0,))
    make_picks()
    have_pair(1, (1,))
    gate_rows(1)
    repeat(theirs, 0, (1,))
    theirs_extra(0, (1,))
    grad_rows(2)
    for n in range(4):
        add(0, (1,), n)
    have_pair(1, (2,))
    gate_rows(2)
    for n in range(NK):
        theirs(0, (2,), n)
        if n == 1:
            for m in range(4, NK):
                add(0, (1,), m)
            add_extra(0, (1,))
    theirs_extra(0, (2,))
    for n in range(NK):
        add(0, (2,), n)
    add_extra(0, (2,))

    def take(b, pick, pos, nb, k):
        at = pl.ds(pos, nb)
        return dot_nn(pick[b, k], jnp.concatenate([
            ret_r[b, at, :, k * C:(k + 1) * C].reshape(16 * nb, C), ret_r[b, at, :, D:].reshape(16 * nb, C)], axis=0))

    def take0(b, k):
        return take(b, pick0, 0, early, k)

    def take1(b, k):
        return take(b, pick1, early, NZ - early, k)

    share_fwd = column(meta_r[1, 2:3, :])
    r = inv_rms(shp.at[1])
    ret_all(1, NZ, 2).wait_recv()
    for k in range(4):
        ks = slice(k * C, (k + 1) * C)
        outs[1, :, ks] = (shp[2, :, ks].astype(F32) + share_fwd * (take0(1, k) + take1(1, k))).astype(BF16)
    out_f = pltpu.make_async_copy(outs.at[1], nf.at[0], osem.at[0])
    out_f.start()

    ret_all(0, early, 0).wait_recv()
    for k in range(4):
        qbuf[:, k * C:(k + 1) * C] = take0(0, k)
    for j in range(3):
        z_all(j).wait_send()
        relay_all(j, NZ, 0).wait_send()
        weight_copies[j].wait_send()
    for b in range(2):
        remote(part_s.at[b], part_r.at[b], ps.at[b], pr.at[0, 0], tok).wait_send()
        ret_all(b, NZ, 0).wait_send()
    ret_all(0, NZ - early, 1).wait_recv()
    total = jnp.zeros((T, 1), F32)
    for k in range(4):
        ks = slice(k * C, (k + 1) * C)
        q = gain_r[0:1, ks] * (qbuf[:, ks] + take1(0, k))
        qbuf[:, ks] = q
        total = total + jnp.sum(shp[1, :, ks].astype(F32) * q, axis=1, keepdims=True)
    coef = r * r * r * (total / D)
    for k in range(4):
        ks = slice(k * C, (k + 1) * C)
        outs[0, :, ks] = (
            shp[0, :, ks].astype(F32) + (r * qbuf[:, ks] - shp[1, :, ks].astype(F32) * coef)).astype(BF16)
        pltpu.make_async_copy(outs.at[0, :, pl.ds(k * C, C)], nb.at[0, :, pl.ds(k * C, C)], osem.at[1]).start()

    out_f.wait()
    pltpu.make_async_copy(outs.at[0], nb.at[0], osem.at[1]).wait()


def settle(nf, nb, nf_out, nb_out, held, sem_in, sem_out):
    into, out = [], []
    for n, (src, dst) in enumerate(((nf, nf_out), (nb, nb_out))):
        for m in range(4):
            at = pl.ds(32 * m, 32)
            into.append(pltpu.make_async_copy(src.at[0, at], held.at[n, at], sem_in.at[n, m]))
            out.append(pltpu.make_async_copy(held.at[n, at], dst.at[0, at], sem_out.at[n, m]))
    for c in into:
        c.start()
    for c, d in zip(into, out):
        c.wait()
        d.start()
    for d in out:
        d.wait()


def per_device(fin, froute, fshare, bin_, bgrad, broute, bshare, gain, gate, up, down):
    vm = pl.BlockSpec(memory_space=pltpu.VMEM)
    hbm = pl.BlockSpec(memory_space=pl.ANY)
    dma = pltpu.SemaphoreType.DMA
    out = jax.ShapeDtypeStruct((1, T, D), BF16)
    v = pltpu.VMEM
    nf, nb = pl.pallas_call(
        kernel,
        out_shape=(out, out),
        in_specs=[hbm, vm, vm, hbm, hbm, vm, vm, vm, hbm, hbm, hbm],
        out_specs=(hbm, hbm),
        scratch_shapes=[
            v((3, T, D), BF16), v((3, T, D), BF16), v((2, 8, T), F32), v((2, 8, T), F32),
            v((8, D), F32), v((8, D), F32),
            v((3, NZ, 16, W), BF16), v((3, NZ, 16, W), BF16), v((3, NZ, 16, W), BF16), v((3, 32 * NG, D), BF16),
            v((D, H), BF16), v((D, H), BF16), v((H, D), BF16),
            v((D, H), BF16), v((D, H), BF16), v((H, D), BF16),
            v((6, 2 * PART, H), F32), v((6, 2 * PART, H), BF16),
            v((2, NZ, 16, W), BF16), v((2, NZ, 16, W), BF16),
            v((2, T, D), F32), v((16 * NG, D), BF16), v((2, 16 * NG, D), F32),
            v((2, NZ, 16, W), BF16), v((2, NZ, 16, W), BF16), v((T, D), F32),
            v((2, 4, T, 192), BF16), v((2, 4, T, 64), BF16), v((2, T, D), BF16),
            dma((9,)), dma((3,)), dma((2,)), dma((NZ,)), dma((3,)), dma((3, NG)),
            dma((3,)), dma((3,)), dma((2,)), dma((1 + NG, NK + 1)),
            dma((2,)), dma((3,)), dma((6,)), dma((6,)), dma((2,)),
        ],
        compiler_params=pltpu.CompilerParams(
            collective_id=1, has_side_effects=True, vmem_limit_bytes=60 << 20
        ),
        name="dualpipe_step",
    )(
        fin, froute.reshape(1, T), fshare.reshape(1, T), bin_, bgrad, broute.reshape(1, T),
        bshare.reshape(1, T), gain, gate, up, down,
    )
    return pl.pallas_call(
        settle,
        out_shape=(out, out),
        in_specs=[pl.BlockSpec(memory_space=pltpu.HBM)] * 2,
        out_specs=(hbm, hbm),
        scratch_shapes=[v((2, T, D), BF16), dma((2, 4)), dma((2, 4))],
        compiler_params=pltpu.CompilerParams(vmem_limit_bytes=60 << 20),
        name="settle",
    )(nf, nb)


def solution(mesh):
    spec = P("pipe", "expert", None)
    return jax.shard_map(
        per_device,
        mesh=mesh,
        in_specs=(
            spec, spec, spec, spec, spec, spec, spec,
            P("pipe", None), P("pipe", None, "expert"), P("pipe", None, "expert"), P("pipe", "expert", None),
        ),
        out_specs=(spec, spec),
        check_vma=False,
    )
```

time: 160 us -> 151 us (0.944)
  Pallas kernels: 156 us -> 150 us
  local copies, waits for them, and re-layouts: 3.17 us -> 0 us
    pallas_call x1, Pallas kernels: 156 us -> 148 us  [per_device(): pl.pallas_call(kernel, out_shape=(out, out), in_specs=[hbm, vm, vm, hbm,...]
    unnamed x4 -> x0, local copies, waits for them, and re-layouts: 3.17 us -> none
    pallas_call x0 -> x1, Pallas kernels: none -> 2.41 us  [per_device(): pl.pallas_call(settle, out_shape=(out, out), in_specs=[pl.BlockSpec(memor...]
where the time goes in v3:
time: 151 us
  Pallas kernels  150 us (99%)
    pallas_call x1, Pallas kernels, per_device(): pl.pallas_call(kernel, out_shape=(out, out), in_specs=[hbm, vm, vm, hbm,...  148 us

profile of v3, /device:TPU:1, one launch (start us, length us, event | category | flops | bytes accessed | tf_op | source)
XLA Modules:
  0.0 151.2 jit_solution(7204955174213573085)
XLA Ops:
  0.6 148.0 %dualpipe_step.1 = (bf16[1,128,3584]{2,1,0:T(8,128)(2,1)}, bf16[1,128,3584]{2,1,0:T(8,128)(2,1)}) custom-call(bf16[1,128,3584]{2,1,0:T(8,128)(2,1)} %fin.1, s32[1,128]{1,0:T(1,128)} %bitcast.4, f32[1,128]{1,0:T(1,128)} %bitcast.5, bf16[1,128,3584]{2,1,0:T(8,128)(2,1)} %bin_.1, bf16[1,128,3584]{2,1,0:T(8,128)(2,1)} %bgrad.1, s32[1,128]{1,0:T(1,128)} %bitcast.6, ...), custom_call_target="tpu_custom_call" | custom-call | tf_op jit(solution)/shard_map/dualpipe_step/pallas_call | solution.py:547
  148.6 2.4 %settle.1 = (bf16[1,128,3584]{2,1,0:T(8,128)(2,1)}, bf16[1,128,3584]{2,1,0:T(8,128)(2,1)}) custom-call(bf16[1,128,3584]{2,1,0:T(8,128)(2,1)} %get-tuple-element.4.nf, bf16[1,128,3584]{2,1,0:T(8,128)(2,1)} %get-tuple-element.5.nb), custom_call_target="tpu_custom_call" | custom-call | tf_op jit(solution)/shard_map/settle/pallas_call | solution.py:575

commit v4 on v3

--- a/solution.py
+++ b/solution.py
@@ -18,7 +18,7 @@
 ORDER = (4, 3, 5, 2, 6, 1, 7)
 NEAR = (1, 7, 2, 6, 3, 5, 4)
 FAR = (4, 3, 5, 2, 6, 1, 7, 0)
-COLS = ((0, 1024), (1024, 1024), (2048, 1024), (3072, 1408))
+COLS = ((0, 512), (512, 1024), (1536, 1024), (2560, 1024), (3584, 896))
 GROUP = ((0, 3), (3, 3), (6, 2))
 NG = len(GROUP)
 ALL = tuple(range(NG))
@@ -79,8 +79,8 @@
     nf, nb,
     xin, shp, meta_s, meta_r, gain_s, gain_r, send, recv, pair, extra,
     gate_o, up_o, down_o, gate_r, up_r, down_r,
-    acc, hid, part_s, part_r, own, eo_b, eo_f, ret_s, ret_r, qbuf, pick0, pick1, outs,
-    lsem, zs, zr, zrf, ys, yr, ws, wr, ps, pr, rs, rr, xs, xr, osem,
+    acc, hid, part_s, part_r, own, eo_b, eo_f, own_ex, ret_s, ret_r, qbuf, pick0, pick1,
+    lsem, zs, zr, zrf, ys, yr, ws, wr, ps, pr, rs, rr, xs, xr,
 ):
     p = lax.axis_index("pipe")
     i = lax.axis_index("expert")
@@ -188,11 +188,11 @@
         remote(down.at[0], down_r, ws.at[2], wr.at[2], wgt),
     ]
 
+    fmain, fextra, ftake, ftake_ex = slots_of(froute[...], z)
+    pack_normed(2, fmain, fextra)
     pl.semaphore_wait(bar, 25)
     for c in weight_copies:
         c.start()
-    fmain, fextra, ftake, ftake_ex = slots_of(froute[...], z)
-    pack_normed(2, fmain, fextra)
     z_send(2)
 
     bmain, bextra, btake, btake_ex = slots_of(broute[...], z)
@@ -305,13 +305,13 @@
         at, h = pl.ds(*span(gs)), 0 if b else 1 + gs[0]
         return remote(part_s.at[b, at, :, ds], part_r.at[b, at, :, ds], ps.at[b], pr.at[h, n], tok)
 
-    def fold_extra(dst, b, gs):
+    def fold_extra(b, gs):
         for g in gs:
             pos, nb = GROUP[g]
             folded = jnp.zeros((16 * nb, C), F32)
             for k in range(4):
                 folded = folded + dot_nn(fold(k, nb), eo_b[16 * g:16 * (g + 1), k * C:(k + 1) * C])
-            dst[b, pos:pos + nb, :, D:] = folded.astype(BF16).reshape(nb, 16, C)
+            part_s[b, pos:pos + nb, :, D:] = folded.astype(BF16).reshape(nb, 16, C)
 
     def theirs(b, gs, n):
         pos, nb = span(gs)
@@ -322,7 +322,7 @@
         part_copy(b, gs, n).start()
 
     def theirs_extra(b, gs):
-        fold_extra(part_s, b, gs)
+        fold_extra(b, gs)
         part_copy(b, gs, NK).start()
 
     def ours(b, gs, n):
@@ -335,7 +335,7 @@
     def ret_copy(b, g, n):
         ds = pl.ds(*COLS[g])
         return remote(ret_s.at[b, n, :, ds], ret_r.at[b, n, :, ds], rs.at[b],
-                      rr.at[2 if b else n // GROUP[-1][0]], at_z(prv if b == 0 else nxt, source(n)))
+                      rr.at[2 if b else min(n // GROUP[0][1], 1)], at_z(prv if b == 0 else nxt, source(n)))
 
     def ret_all(b, nb, h):
         at = pl.ds(0, nb)
@@ -352,20 +352,22 @@
         part_copy(b, gs, n).wait_recv()
         o = own[b, 16 * pos:16 * (pos + nb), ds] + part_r[b, pos:pos + nb, :, ds].reshape(16 * nb, KC).astype(F32)
         ret_s[b, pos:pos + nb, :, ds] = o.astype(BF16).reshape(nb, 16, KC)
-        if n % 2 == 1:
+        if n % 2 == 0:
             ret_send(b, gs, n // 2)
 
+    def fold_own(b):
+        for g, (pos, nb) in enumerate(GROUP):
+            for m in range(nb):
+                for k in range(4):
+                    own_ex[b, 16 * (pos + m) + 4 * k:16 * (pos + m) + 4 * (k + 1), :] = (
+                        eo_f[b, 16 * g + 4 * m:16 * g + 4 * (m + 1), k * C:(k + 1) * C])
+
     def add_extra(b, gs):
+        pos, nb = span(gs)
         part_copy(b, gs, NK).wait_recv()
-        for g in gs:
-            pos, nb = GROUP[g]
-            at = slice(16 * g, 16 * (g + 1))
-            folded = part_r[b, pos:pos + nb, :, D:].reshape(16 * nb, C)
-            for k in range(4):
-                ks = slice(k * C, (k + 1) * C)
-                eo_b[at, ks] = (eo_f[b, at, ks] + dot_nn(unfold(k, nb), folded)).astype(BF16)
-        fold_extra(ret_s, b, gs)
-        ret_send(b, gs, 3)
+        o = own_ex[b, 16 * pos:16 * (pos + nb)] + part_r[b, pos:pos + nb, :, D:].reshape(16 * nb, C).astype(F32)
+        ret_s[b, pos:pos + nb, :, D:] = o.astype(BF16).reshape(nb, 16, C)
+        ret_send(b, gs, 4)
 
     def repeat(fn, b, gs):
         def step(n, _):
@@ -385,7 +387,7 @@
     def names(g):
         return FAR[GROUP[g][0]:GROUP[g][0] + GROUP[g][1]]
 
-    early = span((0, 1))[1]
+    early = GROUP[0][1]
 
     def make_picks():
         for c in ship:
@@ -435,22 +437,27 @@
     keep(1).wait()
     first(1, OWN, ALL, gate_up)
     ours(1, ALL, 6)
+    fold_own(1)
     add(1, ALL, 6)
     add_extra(1, ALL)
     act(act_back, OWN, ALL)
     repeat(ours, 0, ALL)
+    fold_own(0)
     grad_rows(0)
     have_pair(1, (0,))
     gate_rows(0)
-    repeat(theirs, 0, (0,))
+    for n in range(NK):
+        theirs(0, (0,), n)
+        if n == 5:
+            add(0, (0,), 0)
     theirs_extra(0, (0,))
     relay(1, names(1))
     relay(0, names(2))
     relay(1, names(2))
-    add(0, (0,), 0)
-    add(0, (0,), 1)
+    for n in range(1, 3):
+        add(0, (0,), n)
     grad_rows(1)
-    for n in range(2, NK):
+    for n in range(3, NK):
         add(0, (0,), n)
     add_extra(0, (0,))
     make_picks()
@@ -490,9 +497,7 @@
     ret_all(1, NZ, 2).wait_recv()
     for k in range(4):
         ks = slice(k * C, (k + 1) * C)
-        outs[1, :, ks] = (shp[2, :, ks].astype(F32) + share_fwd * (take0(1, k) + take1(1, k))).astype(BF16)
-    out_f = pltpu.make_async_copy(outs.at[1], nf.at[0], osem.at[0])
-    out_f.start()
+        nf[0, :, ks] = (shp[2, :, ks].astype(F32) + share_fwd * (take0(1, k) + take1(1, k))).astype(BF16)
 
     ret_all(0, early, 0).wait_recv()
     for k in range(4):
@@ -514,41 +519,20 @@
     coef = r * r * r * (total / D)
     for k in range(4):
         ks = slice(k * C, (k + 1) * C)
-        outs[0, :, ks] = (
+        nb[0, :, ks] = (
             shp[0, :, ks].astype(F32) + (r * qbuf[:, ks] - shp[1, :, ks].astype(F32) * coef)).astype(BF16)
-        pltpu.make_async_copy(outs.at[0, :, pl.ds(k * C, C)], nb.at[0, :, pl.ds(k * C, C)], osem.at[1]).start()
-
-    out_f.wait()
-    pltpu.make_async_copy(outs.at[0], nb.at[0], osem.at[1]).wait()
-
-
-def settle(nf, nb, nf_out, nb_out, held, sem_in, sem_out):
-    into, out = [], []
-    for n, (src, dst) in enumerate(((nf, nf_out), (nb, nb_out))):
-        for m in range(4):
-            at = pl.ds(32 * m, 32)
-            into.append(pltpu.make_async_copy(src.at[0, at], held.at[n, at], sem_in.at[n, m]))
-            out.append(pltpu.make_async_copy(held.at[n, at], dst.at[0, at], sem_out.at[n, m]))
-    for c in into:
-        c.start()
-    for c, d in zip(into, out):
-        c.wait()
-        d.start()
-    for d in out:
-        d.wait()
 
 
 def per_device(fin, froute, fshare, bin_, bgrad, broute, bshare, gain, gate, up, down):
     vm = pl.BlockSpec(memory_space=pltpu.VMEM)
     hbm = pl.BlockSpec(memory_space=pl.ANY)
     dma = pltpu.SemaphoreType.DMA
-    out = jax.ShapeDtypeStruct((1, T, D), BF16)
     v = pltpu.VMEM
-    nf, nb = pl.pallas_call(
+    return pl.pallas_call(
         kernel,
-        out_shape=(out, out),
+        out_shape=(v((1, T, D), BF16), v((1, T, D), BF16)),
         in_specs=[hbm, vm, vm, hbm, hbm, vm, vm, vm, hbm, hbm, hbm],
-        out_specs=(hbm, hbm),
+        out_specs=(vm, vm),
         scratch_shapes=[
             v((3, T, D), BF16), v((3, T, D), BF16), v((2, 8, T), F32), v((2, 8, T), F32),
             v((8, D), F32), v((8, D), F32),
@@ -557,12 +541,12 @@
             v((D, H), BF16), v((D, H), BF16), v((H, D), BF16),
             v((6, 2 * PART, H), F32), v((6, 2 * PART, H), BF16),
             v((2, NZ, 16, W), BF16), v((2, NZ, 16, W), BF16),
-            v((2, T, D), F32), v((16 * NG, D), BF16), v((2, 16 * NG, D), F32),
+            v((2, T, D), F32), v((16 * NG, D), BF16), v((2, 16 * NG, D), F32), v((2, T, C), F32),
             v((2, NZ, 16, W), BF16), v((2, NZ, 16, W), BF16), v((T, D), F32),
-            v((2, 4, T, 192), BF16), v((2, 4, T, 64), BF16), v((2, T, D), BF16),
+            v((2, 4, T, 96), BF16), v((2, 4, T, 160), BF16),
             dma((9,)), dma((3,)), dma((2,)), dma((NZ,)), dma((3,)), dma((3, NG)),
             dma((3,)), dma((3,)), dma((2,)), dma((1 + NG, NK + 1)),
-            dma((2,)), dma((3,)), dma((6,)), dma((6,)), dma((2,)),
+            dma((2,)), dma((3,)), dma((6,)), dma((6,)),
         ],
         compiler_params=pltpu.CompilerParams(
             collective_id=1, has_side_effects=True, vmem_limit_bytes=60 << 20
@@ -572,15 +556,6 @@
         fin, froute.reshape(1, T), fshare.reshape(1, T), bin_, bgrad, broute.reshape(1, T),
         bshare.reshape(1, T), gain, gate, up, down,
     )
-    return pl.pallas_call(
-        settle,
-        out_shape=(out, out),
-        in_specs=[pl.BlockSpec(memory_space=pltpu.HBM)] * 2,
-        out_specs=(hbm, hbm),
-        scratch_shapes=[v((2, T, D), BF16), dma((2, 4)), dma((2, 4))],
-        compiler_params=pltpu.CompilerParams(vmem_limit_bytes=60 << 20),
-        name="settle",
-    )(nf, nb)
 
 
 def solution(mesh):

time: 151 us -> 151 us (level)
  Pallas kernels: 150 us -> 148 us
  local copies, waits for them, and re-layouts: 0 us -> 1.85 us
    pallas_call x2 -> x1, Pallas kernels: 150 us -> 148 us  [per_device(): pl.pallas_call(kernel, out_shape=(v((1, T, D), BF16), v((1, T, D), BF16))...]
    unnamed x0 -> x2, local copies, waits for them, and re-layouts: none -> 1.85 us
where the time goes in v4:
time: 151 us; the launch traced here: 150 us
  Pallas kernels  148 us (98%)
  local copies, waits for them, and re-layouts  1.85 us (1%)
    pallas_call x1, Pallas kernels, per_device(): pl.pallas_call(kernel, out_shape=(v((1, T, D), BF16), v((1, T, D), BF16))...  148 us

profile of v4, /device:TPU:1, one launch (start us, length us, event | category | flops | bytes accessed | tf_op | source)
XLA Modules:
  0.0 150.4 jit_solution(9194756781428288864)
XLA Ops:
  0.6 147.9 %dualpipe_step.1 = (bf16[1,128,3584]{2,1,0:T(8,128)(2,1)S(1)}, bf16[1,128,3584]{2,1,0:T(8,128)(2,1)S(1)}) custom-call(bf16[1,128,3584]{2,1,0:T(8,128)(2,1)} %fin.1, s32[1,128]{1,0:T(1,128)} %bitcast.4, f32[1,128]{1,0:T(1,128)} %bitcast.5, bf16[1,128,3584]{2,1,0:T(8,128)(2,1)} %bin_.1, bf16[1,128,3584]{2,1,0:T(8,128)(2,1)} %bgrad.1, s32[1,128]{1,0:T(1,128)} %bitcast.6, ...), custom_call_target="tpu_custom_call" | custom-call | tf_op jit(solution)/shard_map/dualpipe_step/pallas_call | solution.py:531
  148.5 0.9 copy.15
  149.5 0.9 copy.16

commit v5 on v4

--- a/solution.py
+++ b/solution.py
@@ -14,6 +14,7 @@
 H = 256
 KC = 512
 NK = D // KC
+K1 = 1792
 F32, BF16 = jnp.float32, jnp.bfloat16
 ORDER = (4, 3, 5, 2, 6, 1, 7)
 NEAR = (1, 7, 2, 6, 3, 5, 4)
@@ -251,7 +252,7 @@
             acc[m, at_ex] = jnp.zeros((16 * len(gs), H), F32)
 
         def step(n, _):
-            ds = pl.ds(pl.multiple_of(n * KC, KC), KC)
+            ds = pl.ds(pl.multiple_of(n * K1, K1), K1)
             v = jnp.concatenate(blocks(pos, nb, ds) + [extra[j, es, ds]], axis=0)
             for m, w, transposed in mats:
                 o = dot_nt(v, w[:, ds]) if transposed else dot_nn(v, w[ds, :])
@@ -259,7 +260,7 @@
                 acc[m, at_ex] += o[16 * nb:]
             return 0
 
-        lax.fori_loop(0, NK, step, 0)
+        lax.fori_loop(0, D // K1, step, 0)
 
     def have_pair(j, gs):
         relay_all(j, span(gs)[1], gs[0]).wait_recv()

time: 151 us -> 149 us (0.987)
  no operation moved by 1% of the time
where the time goes in v5:
time: 149 us
  Pallas kernels  147 us (99%)
  local copies, waits for them, and re-layouts  1.85 us (1%)
    pallas_call x1, Pallas kernels, per_device(): pl.pallas_call(kernel, out_shape=(v((1, T, D), BF16), v((1, T, D), BF16))...  147 us

profile of v5, /device:TPU:1, one launch (start us, length us, event | category | flops | bytes accessed | tf_op | source)
XLA Modules:
  0.0 149.3 jit_solution(11682563747463761907)
XLA Ops:
  0.6 146.8 %dualpipe_step.1 = (bf16[1,128,3584]{2,1,0:T(8,128)(2,1)S(1)}, bf16[1,128,3584]{2,1,0:T(8,128)(2,1)S(1)}) custom-call(bf16[1,128,3584]{2,1,0:T(8,128)(2,1)} %fin.1, s32[1,128]{1,0:T(1,128)} %bitcast.4, f32[1,128]{1,0:T(1,128)} %bitcast.5, bf16[1,128,3584]{2,1,0:T(8,128)(2,1)} %bin_.1, bf16[1,128,3584]{2,1,0:T(8,128)(2,1)} %bgrad.1, s32[1,128]{1,0:T(1,128)} %bitcast.6, ...), custom_call_target="tpu_custom_call" | custom-call | tf_op jit(solution)/shard_map/dualpipe_step/pallas_call | solution.py:532
  147.5 0.9 copy.15
  148.4 0.9 copy.16
